TPU v7x, 32 devices: a whole 2x2x4 slice. The times are simulated.
32 devices in a mesh: pix: 8 (over z, y), chan: 4 (over x, core).
Axes of the slice: x: 2, y: 2, z: 4, core: 2. Of those that a mesh axis runs over, the one named last changes fastest.
Arguments:
- spectra: bfloat16 [32768, 2048], P('pix', 'chan'), may hold values from 0.05 to 2100, as said below
- start: bfloat16 [64, 2048], P(None, 'chan'), may hold values from -6 to 6
- anchors: int32 [16], replicated, may hold values from 0 to 32767, as said below
Outputs:
- scores: float32 [64, 32768], P(None, 'pix')
- abundance: float32 [16, 32768], P(None, 'pix')
Inputs may be any that keep to these rules, and one draw needn't show every extreme that they name: `spectra`: every entry is positive. `anchors`: the 16 indices are distinct; pixel 0 and pixel 32768 - 1 are among them.
All inputs are finite; a program needn't handle non-finite values.
Results may differ from a plain program's by a relative error of at most 0.035.
Values may be sent and summed in bfloat16 or wider, within the bound.
A program may use at most 64 MiB of HBM per device.

v0:
```python
import jax
import jax.numpy as jnp
from jax import lax
from jax.sharding import PartitionSpec as P

ITERS = 5


def tri_solve(lower, rhs):
    return lax.linalg.triangular_solve(lower, rhs, left_side=True, lower=True)


def project(loadings, weighted):
    return lax.dot_general(
        loadings, weighted, (((1,), (1,)), ((), ())), preferred_element_type=jnp.float32
    )


def local(spectra, start, anchors):
    pix_rows = spectra.shape[0]
    col_part = jnp.sum(spectra, axis=0, dtype=jnp.float32)
    colsum = lax.psum(col_part, "pix")
    row_part = jnp.sum(spectra, axis=1, dtype=jnp.float32)
    rowsum, total = lax.psum((row_part, jnp.sum(colsum)), "chan")
    expect = rowsum[:, None] * colsum[None, :] / total
    weighted = ((spectra.astype(jnp.float32) - expect) * lax.rsqrt(expect)).astype(jnp.bfloat16)
    loadings = start
    for step in range(ITERS):
        partial_proj = project(loadings, weighted).astype(jnp.bfloat16)
        proj = lax.psum(partial_proj, "chan").astype(jnp.float32).astype(jnp.bfloat16)
        back = jnp.dot(proj, weighted, preferred_element_type=jnp.float32)
        full = lax.psum(back, "pix")
        gram = lax.psum(jnp.dot(full, full.T, precision=lax.Precision.HIGHEST), "chan")
        lower = jnp.linalg.cholesky(gram)
        renewed = tri_solve(lower, full)
        loadings = renewed.astype(jnp.bfloat16)
    score_part = project(loadings, weighted)
    scores = lax.psum(score_part.astype(jnp.bfloat16), "chan").astype(jnp.float32)
    offset = lax.axis_index("pix") * pix_rows
    positions = lax.broadcasted_iota(jnp.int32, (anchors.shape[0], pix_rows), 1)
    picks = (anchors[:, None] - offset == positions).astype(jnp.float32)
    contract = (((1,), (1,)), ((), ()))
    local_rows = lax.dot_general(picks, scores, contract, precision=lax.Precision.HIGHEST)
    rows = lax.psum(local_rows, "pix")
    small = jnp.dot(rows, rows.T, precision=lax.Precision.HIGHEST)
    lower = jnp.linalg.cholesky(small)
    rhs = jnp.dot(rows, scores, precision=lax.Precision.HIGHEST)
    middle = tri_solve(lower, rhs)
    abundance = lax.linalg.triangular_solve(
        lower, middle, left_side=True, lower=True, transpose_a=True
    )
    return (scores, abundance)


def solution(mesh):
    placed = (P("pix", "chan"), P(None, "chan"), P())
    return jax.shard_map(
        local,
        mesh=mesh,
        in_specs=placed,
        out_specs=(P(None, "pix"), P(None, "pix")),
        check_vma=False,
    )
```

profile of v0, /device:TPU:0, one launch (start us, length us, event | category | flops | bytes accessed | tf_op | source)
XLA Modules:
  0.0 804.8 jit_solution(3142120066821343454)
XLA Ops:
  7.2 3.5 convert_reduce_fusion.1
  10.8 23.1 %psum.141 = f32[512]{0:T(512)S(1)} all-reduce(f32[512]{0:T(512)S(1)} %get-tuple-element.5), channel_id=1, replica_groups=mesh['pix'=8,'chan'=4] {'pix'}, use_global_device_ids=true, to_apply=%region_3.0 | all-reduce | flops 512 | bytes 4096 | tf_op jit(solution)/shard_map/psum | solution.py:22
  34.5 11.3 %all-reduce = (f32[]{:T(128)}, f32[4096]{0:T(1024)S(1)}) all-reduce(f32[]{:T(128)} %reduce_sum.29, f32[4096]{0:T(1024)S(1)} %get-tuple-element.4), channel_id=1, replica_groups=mesh['pix'=8,'chan'=4] {'chan'}, use_global_device_ids=true, to_apply=%region_5.0 | all-reduce | flops 4097 | bytes 32776 | tf_op jit(solution)/shard_map/psum | solution.py:24
  45.8 4.2 fusion.1
  49.9 1.9 copy-done.1
  51.9 2.2 fusion.2
  54.1 32.4 %all-reduce.13.cloned.1.call-done = bf16[64,4096]{0,1:T(8,128)(2,1)} async-done(((bf16[64,4096]{0,1:T(8,128)(2,1)}), bf16[64,4096]{0,1:T(8,128)(2,1)}) %all-reduce.13.cloned.1.call-update) | async-done | bytes 524304 | tf_op jit(solution)/shard_map/psum | solution.py:30
  86.6 4.0 fusion.34
  90.7 70.2 %all-reduce.15.cloned.1.call-done = f32[64,512]{1,0:T(8,128)} async-done(((f32[64,512]{1,0:T(8,128)}), f32[64,512]{1,0:T(8,128)}) %all-reduce.15.cloned.1.call-update) | async-done | bytes 131088 | tf_op jit(solution)/shard_map/psum | solution.py:32
  160.9 1.2 fusion.35
  162.1 10.3 %psum.145 = f32[64,64]{0,1:T(8,128)S(1)} all-reduce(f32[64,64]{0,1:T(8,128)S(1)} %fusion.35), channel_id=1, replica_groups=mesh['pix'=8,'chan'=4] {'chan'}, use_global_device_ids=true, to_apply=%region_8.0 | all-reduce | flops 4096 | bytes 32768 | tf_op jit(solution)/shard_map/psum | solution.py:33
  172.5 5.8 cholesky.124
  179.0 0.7 fusion.5
  179.7 4.9 custom-call.18
  184.6 1.2 convolution_convert_fusion.10
  185.8 4.4 convolution_convert_fusion.5
  190.3 32.7 %all-reduce.17.cloned.1.call-done = bf16[64,4096]{1,0:T(8,128)(2,1)} async-done(((bf16[64,4096]{1,0:T(8,128)(2,1)}), bf16[64,4096]{1,0:T(8,128)(2,1)}) %all-reduce.17.cloned.1.call-update) | async-done | bytes 524304 | tf_op jit(solution)/shard_map/psum | solution.py:30
  223.0 3.8 fusion.36
  226.9 69.7 %all-reduce.19.cloned.1.call-done = f32[64,512]{1,0:T(8,128)} async-done(((f32[64,512]{1,0:T(8,128)}), f32[64,512]{1,0:T(8,128)}) %all-reduce.19.cloned.1.call-update) | async-done | bytes 131088 | tf_op jit(solution)/shard_map/psum | solution.py:32
  296.6 1.2 fusion.37
  297.9 10.3 %psum.148 = f32[64,64]{0,1:T(8,128)S(1)} all-reduce(f32[64,64]{0,1:T(8,128)S(1)} %fusion.37), channel_id=1, replica_groups=mesh['pix'=8,'chan'=4] {'chan'}, use_global_device_ids=true, to_apply=%region_13.16 | all-reduce | flops 4096 | bytes 32768 | tf_op jit(solution)/shard_map/psum | solution.py:33
  308.2 5.8 cholesky.135
  314.8 0.7 fusion.6
  315.4 4.9 custom-call.19
  320.3 1.2 convolution_convert_fusion.9
  321.6 4.4 convolution_convert_fusion.4
  326.0 32.7 %all-reduce.21.cloned.1.call-done = bf16[64,4096]{1,0:T(8,128)(2,1)} async-done(((bf16[64,4096]{1,0:T(8,128)(2,1)}), bf16[64,4096]{1,0:T(8,128)(2,1)}) %all-reduce.21.cloned.1.call-update) | async-done | bytes 524304 | tf_op jit(solution)/shard_map/psum | solution.py:30
  358.7 3.8 fusion.38
  362.8 69.7 %all-reduce.23.cloned.1.call-done = f32[64,512]{1,0:T(8,128)} async-done(((f32[64,512]{1,0:T(8,128)}), f32[64,512]{1,0:T(8,128)}) %all-reduce.23.cloned.1.call-update) | async-done | bytes 131088 | tf_op jit(solution)/shard_map/psum | solution.py:32
  432.5 1.2 fusion.39
  433.7 10.3 %psum.151 = f32[64,64]{0,1:T(8,128)S(1)} all-reduce(f32[64,64]{0,1:T(8,128)S(1)} %fusion.39), channel_id=1, replica_groups=mesh['pix'=8,'chan'=4] {'chan'}, use_global_device_ids=true, to_apply=%region_16.19 | all-reduce | flops 4096 | bytes 32768 | tf_op jit(solution)/shard_map/psum | solution.py:33
  444.1 5.8 cholesky.146
  450.6 0.7 fusion.7
  451.3 4.9 custom-call.20
  456.2 1.2 convolution_convert_fusion.8
  457.4 4.4 convolution_convert_fusion.3
  461.9 32.7 %all-reduce.25.cloned.1.call-done = bf16[64,4096]{1,0:T(8,128)(2,1)} async-done(((bf16[64,4096]{1,0:T(8,128)(2,1)}), bf16[64,4096]{1,0:T(8,128)(2,1)}) %all-reduce.25.cloned.1.call-update) | async-done | bytes 524304 | tf_op jit(solution)/shard_map/psum | solution.py:30
  494.6 3.8 fusion.40
  498.5 69.7 %all-reduce.27.cloned.1.call-done = f32[64,512]{1,0:T(8,128)} async-done(((f32[64,512]{1,0:T(8,128)}), f32[64,512]{1,0:T(8,128)}) %all-reduce.27.cloned.1.call-update) | async-done | bytes 131088 | tf_op jit(solution)/shard_map/psum | solution.py:32
  568.2 1.2 fusion.41
  569.4 10.3 %psum.154 = f32[64,64]{0,1:T(8,128)S(1)} all-reduce(f32[64,64]{0,1:T(8,128)S(1)} %fusion.41), channel_id=1, replica_groups=mesh['pix'=8,'chan'=4] {'chan'}, use_global_device_ids=true, to_apply=%region_19.22 | all-reduce | flops 4096 | bytes 32768 | tf_op jit(solution)/shard_map/psum | solution.py:33
  579.8 5.8 cholesky.157
  586.3 0.7 fusion.8
  587.0 4.9 custom-call.21
  591.9 1.2 convolution_convert_fusion.7
  593.1 4.4 convolution_convert_fusion.2
  597.6 32.7 %all-reduce.29.cloned.1.call-done = bf16[64,4096]{1,0:T(8,128)(2,1)} async-done(((bf16[64,4096]{1,0:T(8,128)(2,1)}), bf16[64,4096]{1,0:T(8,128)(2,1)}) %all-reduce.29.cloned.1.call-update) | async-done | bytes 524304 | tf_op jit(solution)/shard_map/psum | solution.py:30
  630.3 3.8 fusion.42
  634.2 69.8 %all-reduce.31.cloned.1.call-done = f32[64,512]{1,0:T(8,128)} async-done(((f32[64,512]{1,0:T(8,128)}), f32[64,512]{1,0:T(8,128)}) %all-reduce.31.cloned.1.call-update) | async-done | bytes 131088 | tf_op jit(solution)/shard_map/psum | solution.py:32
  704.0 1.2 fusion.43
  705.3 10.3 %psum.157 = f32[64,64]{0,1:T(8,128)S(1)} all-reduce(f32[64,64]{0,1:T(8,128)S(1)} %fusion.43), channel_id=1, replica_groups=mesh['pix'=8,'chan'=4] {'chan'}, use_global_device_ids=true, to_apply=%region_22.25 | all-reduce | flops 4096 | bytes 32768 | tf_op jit(solution)/shard_map/psum | solution.py:33
  715.6 5.8 cholesky.168
  722.2 0.7 fusion.9
  722.8 4.9 custom-call.22
  727.7 1.2 convolution_convert_fusion.6
  728.9 4.4 convolution_convert_fusion.1
  733.4 32.8 %all-reduce.33.cloned.1.call-done = bf16[64,4096]{1,0:T(8,128)(2,1)} async-done(((bf16[64,4096]{1,0:T(8,128)(2,1)}), bf16[64,4096]{1,0:T(8,128)(2,1)}) %all-reduce.33.cloned.1.call-update) | async-done | bytes 524304 | tf_op jit(solution)/shard_map/psum | solution.py:38
  766.1 1.3 fusion.3
  767.5 21.6 %psum.159 = f32[16,64]{1,0:T(8,128)S(1)} all-reduce(f32[16,64]{1,0:T(8,128)S(1)} %fusion.3), channel_id=1, replica_groups=mesh['pix'=8,'chan'=4] {'pix'}, use_global_device_ids=true, to_apply=%region_24.27 | all-reduce | flops 1024 | bytes 8192 | tf_op jit(solution)/shard_map/psum | solution.py:44
  789.3 1.5 cholesky.41
  792.1 1.2 custom-call.13
  793.3 1.4 fusion.45
  795.1 1.1 fusion.29
  796.2 2.1 convert_element_type.72
  (56 shorter events, 7.2 us)
Async XLA Ops:
  7.2 44.7 %copy-start = (bf16[64,512]{1,0:T(8,128)(2,1)S(1)}, bf16[64,512]{1,0:T(8,128)(2,1)}, u32[]{:S(2)}) copy-start(bf16[64,512]{1,0:T(8,128)(2,1)} %param.7) | copy-start | bytes 196612
  7.2 79.4 %all-reduce.13.cloned.1.call-start = ((), (), s32[]{:S(2)}) async-start(), calls=%async_computation | async-start | bytes 2097152 | tf_op jit(solution)/shard_map/psum | solution.py:30
  49.9 1.9 copy-start.1
  54.1 106.8 %all-reduce.15.cloned.1.call-start = ((), (), s32[]{:S(2)}) async-start(), calls=%async_computation.1 | async-start | bytes 262144 | tf_op jit(solution)/shard_map/psum | solution.py:32
  90.6 132.3 %all-reduce.17.cloned.1.call-start = ((), (), s32[]{:S(2)}) async-start(), calls=%async_computation.2 | async-start | bytes 1048576 | tf_op jit(solution)/shard_map/psum | solution.py:30
  190.2 106.4 %all-reduce.19.cloned.1.call-start = ((), (), s32[]{:S(2)}) async-start(), calls=%async_computation.3 | async-start | bytes 262144 | tf_op jit(solution)/shard_map/psum | solution.py:32
  226.9 131.9 %all-reduce.21.cloned.1.call-start = ((), (), s32[]{:S(2)}) async-start(), calls=%async_computation.4 | async-start | bytes 1048576 | tf_op jit(solution)/shard_map/psum | solution.py:30
  325.9 106.5 %all-reduce.23.cloned.1.call-start = ((), (), s32[]{:S(2)}) async-start(), calls=%async_computation.5 | async-start | bytes 262144 | tf_op jit(solution)/shard_map/psum | solution.py:32
  362.6 132.0 %all-reduce.25.cloned.1.call-start = ((), (), s32[]{:S(2)}) async-start(), calls=%async_computation.6 | async-start | bytes 1048576 | tf_op jit(solution)/shard_map/psum | solution.py:30
  461.8 106.4 %all-reduce.27.cloned.1.call-start = ((), (), s32[]{:S(2)}) async-start(), calls=%async_computation.7 | async-start | bytes 262144 | tf_op jit(solution)/shard_map/psum | solution.py:32
  498.4 131.8 %all-reduce.29.cloned.1.call-start = ((), (), s32[]{:S(2)}) async-start(), calls=%async_computation.8 | async-start | bytes 1048576 | tf_op jit(solution)/shard_map/psum | solution.py:30
  597.5 106.5 %all-reduce.31.cloned.1.call-start = ((), (), s32[]{:S(2)}) async-start(), calls=%async_computation.9 | async-start | bytes 262144 | tf_op jit(solution)/shard_map/psum | solution.py:32
  634.1 99.2 %copy-start.2 = (s32[16]{0:T(128)S(1)}, s32[16]{0:T(128)}, u32[]{:S(2)}) copy-start(s32[16]{0:T(128)} %param.8) | copy-start | bytes 196
  634.1 132.0 %all-reduce.33.cloned.1.call-start = ((), (), s32[]{:S(2)}) async-start(), calls=%async_computation.10 | async-start | bytes 1048576 | tf_op jit(solution)/shard_map/psum | solution.py:38
Sparse Core Ops, SparseCore 0:
  54.2 32.3 all-reduce.12
  90.9 69.9 all-reduce.14
  190.3 32.6 all-reduce.16
  227.0 69.5 all-reduce.18
  326.1 32.6 all-reduce.20
  362.9 69.5 all-reduce.22
  461.9 32.5 all-reduce.24
  498.6 69.5 all-reduce.26
  597.6 32.5 all-reduce.28
  634.4 69.5 all-reduce.30
  733.5 32.6 all-reduce.32
where the time goes:
time: 806 us; the launch traced here: 805 us
  waiting for transfers between devices  545 us (68%)
  blocking collectives  107 us (13%)
  other arithmetic  74.8 us (9%)
  matrix products  60.1 us (7%)
  between operations  14.2 us (2%)
    psum x5, waiting for transfers between devices, local(): full = lax.psum(back, 'pix')  349 us
    psum x5, waiting for transfers between devices, local(): lax.psum(partial_proj, 'chan').astype(jnp.float32).astype(jnp.bfloat16)  163 us
    psum x5, blocking collectives, local(): lax.psum(jnp.dot(full, full.T, precision=lax.Precision.HIGHEST), 'chan')  51.3 us
    psum x1, waiting for transfers between devices, local(): lax.psum(score_part.astype(jnp.bfloat16), 'chan').astype(jnp.float32)  32.8 us
    another operation x15, other arithmetic, local(): lower = jnp.linalg.cholesky(gram)  32.6 us
    another operation x10, other arithmetic, tri_solve(): return lax.linalg.triangular_solve(lower, rhs, left_side=True, lower=True)  27.7 us
    dot_general x6, matrix products, project(): lax.dot_general(loadings, weighted, (((1,), (1,)), ((), ())), preferred_e...  24 us
    psum x1, blocking collectives, local(): colsum = lax.psum(col_part, 'pix')  23.1 us
  transfers between devices with their start and end apart: 11, of which 11 were waited for; matrix products, arithmetic and copies ran while one was open for 0% of the time, Pallas kernels for 0%

commit v1 on v0

v1 whole, which is shorter than its diff:
```python
import functools

import jax
import jax.numpy as jnp
from jax import lax
from jax.experimental import pallas as pl
from jax.experimental.pallas import tpu as pltpu
from jax.sharding import PartitionSpec as P

ITERS = 5
GROUP = 8
MESH = pl.DeviceIdType.MESH
HIGH = lax.Precision.HIGHEST
F32 = jnp.float32
BF16 = jnp.bfloat16
NT = (((1,), (1,)), ((), ()))


def dot(a, b, dims=(((1,), (0,)), ((), ())), precision=None):
    return lax.dot_general(a, b, dims, precision=precision, preferred_element_type=F32)


def inverse_factor(gram):
    n = gram.shape[0]
    rows = lax.broadcasted_iota(jnp.int32, (n, 128), 0)
    lanes = lax.broadcasted_iota(jnp.int32, (n, 128), 1)
    full = jnp.where(lanes == rows, 1.0, gram)
    sub = lax.broadcasted_iota(jnp.int32, (8, 128), 0)
    blocks = [full[8 * i : 8 * i + 8, :] for i in range(n // 8)]
    for k in range(n):
        home, r = k // 8, k % 8
        row = blocks[home][r : r + 1, :]
        scaled = row * (1.0 / row[:, 64 + k : 65 + k])
        for i in range(home, n // 8):
            column = blocks[i][:, 64 + k : 65 + k]
            change = column * scaled
            if i == home:
                change = jnp.where(sub > r, change, 0.0)
            blocks[i] = blocks[i] - change
    full = jnp.concatenate(blocks, axis=0)
    pivots = jnp.sum(jnp.where(lanes == rows + 64, full, 0.0), axis=1, keepdims=True)
    return jnp.where(lanes < 64, full * lax.rsqrt(pivots), 0.0)


def kernel(
    n_pix, s_ref, start_ref, anchors_ref, scores_ref, abund_ref,
    other_s, start_in, col_out, col_in, col_mine, col_chan, row_out, row_in, row_sum,
    w, wt, load, x_out, x_in, acc, half_in, keep, rs_in, hi_in, ag, back_in, padded,
    gram_out, gram_in, score, rows_half, rows_half_in, rows_out, rows_in, rows_pad,
    s_sem, st_sem, col_sem, cc_sem, row_sem, x_sem, half_sem, rs_sem, hi_sem, ag_sem,
    bk_sem, gram_sem, sc_sem, rh_sem, rows_sem,
):
    pix = lax.axis_index("pix")
    chan = lax.axis_index("chan")
    lo, hi = lax.rem(chan, 2), lax.div(chan, 2)
    mates = [hi * 2 + 1 - lo, (1 - hi) * 2 + lo, (1 - hi) * 2 + 1 - lo]
    low = lax.rem(pix, GROUP)
    base = pix - low
    n_hi = n_pix // GROUP
    k_rows, ch = start_ref.shape
    pixels = s_ref.shape[0]
    half = pixels // 2
    step_pix = x_out.shape[-1]
    chunks = half // step_pix

    def send(src, dst, sems, device):
        return pltpu.make_async_remote_copy(
            src_ref=src, dst_ref=dst, send_sem=sems.at[0], recv_sem=sems.at[1],
            device_id=device, device_id_type=MESH,
        )

    def all_pix(f):
        def body(d, carry):
            f(d, lax.rem(pix + d, n_pix))
            return carry
        lax.fori_loop(1, n_pix, body, 0)

    barrier = pltpu.get_barrier_semaphore()
    for mate in mates:
        pl.semaphore_signal(barrier, inc=1, device_id=(pix, mate), device_id_type=MESH)
    all_pix(lambda d, to: pl.semaphore_signal(
        barrier, inc=1, device_id=(to, chan), device_id_type=MESH))
    pl.semaphore_wait(barrier, 3 + n_pix - 1)

    away = pl.multiple_of((1 - lo) * half, half)
    swap = send(s_ref.at[pl.ds(away, half)], other_s, s_sem, (pix, mates[0]))
    swap.start()
    swap_start = send(start_ref, start_in, st_sem, (pix, mates[0]))
    swap_start.start()

    ones = jnp.ones((8, step_pix), BF16)
    total_col = jnp.zeros((8, ch), F32)
    for j in range(2 * chunks):
        total_col += dot(ones, s_ref[j * step_pix : (j + 1) * step_pix, :])
    col_out[...] = total_col

    def col_copy(d, to):
        return send(col_out, col_in.at[d], col_sem.at[d], (to, chan))
    all_pix(lambda d, to: col_copy(d, to).start())

    ones_ch = jnp.ones((8, ch), BF16)
    for j in range(2 * chunks):
        sums = dot(ones_ch, s_ref[j * step_pix : (j + 1) * step_pix, :], NT)
        row_out[j : j + 1, :] = sums[0:1, :]
    row_copies = [
        send(row_out, row_in.at[m], row_sem.at[m], (pix, mates[m])) for m in range(3)
    ]
    for copy in row_copies:
        copy.start()

    col_in[0] = col_out[...]
    all_pix(lambda d, to: col_copy(d, to).wait())
    col_mine[...] = jnp.sum(col_in[...], axis=0)
    col_copies = [
        send(col_mine, col_chan.at[m], cc_sem.at[m], (pix, mates[m])) for m in range(3)
    ]
    for copy in col_copies:
        copy.start()
    for copy in row_copies:
        copy.wait()
    sums = (row_out[...] + row_in[0]) + (row_in[1] + row_in[2])
    for j in range(2 * chunks):
        row_sum[j] = jnp.broadcast_to(sums[j : j + 1, :], (8, step_pix))
    for copy in col_copies:
        copy.wait()
    cols = (col_mine[0:1, :] + col_chan[0, 0:1, :]) + (
        col_chan[1, 0:1, :] + col_chan[2, 0:1, :])
    inv_total = 1.0 / jnp.sum(cols, axis=1, keepdims=True)
    shares = [col_mine[0:1, :] * inv_total, col_chan[0, 0:1, :] * inv_total]
    swap.wait()

    tiles = step_pix // 128

    def weigh(i, carry):
        j, q = lax.div(i, tiles), lax.rem(i, tiles)
        first = pl.multiple_of(q * 128, 128)
        line = row_sum[lo * chunks + j, 0:1, pl.ds(first, 128)]
        wide = jnp.transpose(jnp.broadcast_to(line, (128, 128)))
        mine = s_ref[pl.ds(pl.multiple_of(lo * half + i * 128, 128), 128), :]
        theirs = other_s[pl.ds(pl.multiple_of(i * 128, 128), 128), :]
        for side, counts in enumerate((mine, theirs)):
            for g in range(ch // 128):
                expect = wide * shares[side][:, g * 128 : (g + 1) * 128]
                value = counts[:, g * 128 : (g + 1) * 128].astype(F32)
                weighted = (value - expect) * lax.rsqrt(expect)
                at = side * ch + g * 128
                w[j, pl.ds(first, 128), at : at + 128] = weighted.astype(BF16)
                wt[j, at : at + 128, pl.ds(first, 128)] = jnp.transpose(weighted).astype(BF16)
        return carry
    lax.fori_loop(0, chunks * tiles, weigh, 0)

    swap_start.wait()
    load[:, :ch] = start_ref[...]
    load[:, ch:] = start_in[...]
    padded[...] = jnp.zeros_like(padded)
    rows_pad[...] = jnp.zeros_like(rows_pad)

    def x_copy(t, j):
        return send(x_out.at[t, j], x_in.at[t, j], x_sem.at[t, j], (pix, mates[1]))

    def project(t):
        def body(j, carry):
            x_out[t, j] = dot(load[...], wt[j]).astype(BF16)
            x_copy(t, j).start()
            return carry
        lax.fori_loop(0, chunks, body, 0)

    def gather(t, j):
        x_copy(t, j).wait()
        return x_out[t, j].astype(F32) + x_in[t, j].astype(F32)

    per = k_rows // GROUP

    def iteration(t, carry):
        project(t)
        acc[...] = jnp.zeros_like(acc)

        def body(j, carry):
            acc[...] += dot(gather(t, j).astype(BF16), w[j])
            return carry
        lax.fori_loop(0, chunks, body, 0)

        keep[t, 0] = acc[:, ch:]
        copy = send(keep.at[t, 0], half_in.at[t], half_sem.at[t], (pix, mates[0]))
        copy.start()
        copy.wait()
        keep[t, 1] = acc[:, :ch] + half_in[t]

        def partner(d):
            return lax.rem(low + d, GROUP)
        spread = [
            send(
                keep.at[t, 1, pl.ds(pl.multiple_of(partner(d) * per, per), per)],
                rs_in.at[t, d], rs_sem.at[t, d], (base + partner(d), chan))
            for d in range(1, GROUP)
        ]
        for copy in spread:
            copy.start()
        slab = keep[t, 1, pl.ds(pl.multiple_of(low * per, per), per), :]
        for d, copy in enumerate(spread, 1):
            copy.wait()
            slab = slab + rs_in[t, d]
        if n_hi > 1:
            hi_in[t, 0] = slab
            across = [
                send(hi_in.at[t, 0], hi_in.at[t, e], hi_sem.at[t, e],
                     (lax.rem(pix + e * GROUP, n_pix), chan))
                for e in range(1, n_hi)
            ]
            for copy in across:
                copy.start()
            for copy in across:
                copy.wait()
            slab = hi_in[t, lax.rem(n_hi + lax.div(pix, GROUP), n_hi)]
            for e in range(1, n_hi):
                slab = slab + hi_in[t, lax.rem(n_hi + lax.div(pix, GROUP) - e, n_hi)]
        mine = pl.ds(pl.multiple_of(low * per, per), per)
        ag[t, mine] = slab
        collect = [
            send(ag.at[t, mine], ag.at[t, mine], ag_sem.at[t, d], (base + partner(d), chan))
            for d in range(1, GROUP)
        ]
        for copy in collect:
            copy.start()
        for copy in collect:
            copy.wait()
        twin = send(ag.at[t], back_in.at[t], bk_sem.at[t], (pix, mates[0]))
        twin.start()
        back = ag[t]
        padded[k_rows : 2 * k_rows, :ch] = back
        gram_out[t] = dot(back, padded[: 2 * k_rows, :ch], NT, HIGH)
        grams = [
            send(gram_out.at[t], gram_in.at[t, m], gram_sem.at[t, m], (pix, mates[m]))
            for m in range(3)
        ]
        for copy in grams:
            copy.start()
        for copy in grams:
            copy.wait()
        gram = (gram_out[t] + gram_in[t, 0]) + (gram_in[t, 1] + gram_in[t, 2])
        factor = inverse_factor(gram)
        twin.wait()
        padded[k_rows : 2 * k_rows, ch:] = back_in[t]
        load[...] = dot(factor, padded[k_rows:, :], precision=HIGH).astype(BF16)
        return carry
    lax.fori_loop(0, ITERS, iteration, 0)

    project(ITERS)
    n_anchor = anchors_ref.shape[0]
    wanted = anchors_ref[...][:, :1] - pix * pixels - lo * half
    rows_half[...] = jnp.zeros_like(rows_half)

    def finish(j, carry):
        value = gather(ITERS, j)
        slot = lo * chunks + j
        score[slot] = value
        send(score.at[slot], score.at[slot], sc_sem.at[j], (pix, mates[0])).start()
        positions = lax.broadcasted_iota(jnp.int32, (n_anchor, step_pix), 1)
        picks = jnp.where(positions == wanted - j * step_pix, 1.0, 0.0)
        rows_half[...] += dot(picks, value, NT, HIGH)
        return carry
    lax.fori_loop(0, chunks, finish, 0)
    pair_rows = send(rows_half, rows_half_in, rh_sem, (pix, mates[0]))
    pair_rows.start()
    pair_rows.wait()
    rows_out[...] = rows_half[...] + rows_half_in[...]

    def rows_copy(d, to):
        return send(rows_out, rows_in.at[d], rows_sem.at[d], (to, chan))
    all_pix(lambda d, to: rows_copy(d, to).start())
    rows_in[0] = rows_out[...]
    for j in range(chunks):
        slot = lo * chunks + j
        send(score.at[slot], score.at[slot], sc_sem.at[j], (pix, mates[0])).wait()
    for j in range(2 * chunks):
        scores_ref[:, j * step_pix : (j + 1) * step_pix] = score[j]
    all_pix(lambda d, to: rows_copy(d, to).wait())
    rows = jnp.sum(rows_in[...], axis=0)
    rows_pad[64 : 64 + n_anchor, :] = rows
    small = dot(rows, rows_pad[0:128, :], NT, HIGH)
    factor = inverse_factor(small)
    solved = dot(factor, rows_pad[64:192, :], precision=HIGH)
    both = dot(jnp.transpose(factor)[:n_anchor, :], solved, precision=HIGH)
    for j in range(2 * chunks):
        abund_ref[:, j * step_pix : (j + 1) * step_pix] = dot(both, score[j], precision=HIGH)


def local(n_pix, spectra, start, anchors):
    pixels, ch = spectra.shape
    k = start.shape[0]
    na = anchors.shape[0]
    half = pixels // 2
    step = min(512, half)
    chunks = half // step
    n_hi = n_pix // GROUP
    spread = jnp.broadcast_to(anchors[:, None], (na, 128))
    vmem = pl.BlockSpec(memory_space=pltpu.VMEM)
    v = pltpu.VMEM
    sem = lambda *shape: pltpu.SemaphoreType.DMA(tuple(shape) + (2,))
    scratch = [
        v((half, ch), BF16), v((k, ch), BF16), v((8, ch), F32), v((n_pix, 8, ch), F32),
        v((8, ch), F32), v((3, 8, ch), F32), v((2 * chunks, step), F32),
        v((3, 2 * chunks, step), F32), v((2 * chunks, 8, step), F32),
        v((chunks, step, 2 * ch), BF16), v((chunks, 2 * ch, step), BF16), v((k, 2 * ch), BF16),
        v((ITERS + 1, chunks, k, step), BF16), v((ITERS + 1, chunks, k, step), BF16),
        v((k, 2 * ch), F32), v((ITERS, k, ch), F32), v((ITERS, 2, k, ch), F32),
        v((ITERS, GROUP, k // GROUP, ch), F32), v((ITERS, n_hi, k // GROUP, ch), F32),
        v((ITERS, k, ch), F32), v((ITERS, k, ch), F32), v((3 * k, 2 * ch), F32),
        v((ITERS, k, 2 * k), F32), v((ITERS, 3, k, 2 * k), F32),
        v((2 * chunks, k, step), F32), v((na, k), F32), v((na, k), F32), v((na, k), F32),
        v((n_pix, na, k), F32), v((192, k), F32),
        sem(), sem(), sem(n_pix), sem(3), sem(3), sem(ITERS + 1, chunks), sem(ITERS),
        sem(ITERS, GROUP), sem(ITERS, n_hi), sem(ITERS, GROUP), sem(ITERS), sem(ITERS, 3),
        sem(chunks), sem(), sem(n_pix),
    ]
    return pl.pallas_call(
        functools.partial(kernel, n_pix),
        out_shape=(
            jax.ShapeDtypeStruct((k, pixels), F32),
            jax.ShapeDtypeStruct((na, pixels), F32),
        ),
        in_specs=[vmem] * 3,
        out_specs=(vmem, vmem),
        scratch_shapes=scratch,
        compiler_params=pltpu.CompilerParams(
            collective_id=0, has_side_effects=True, vmem_limit_bytes=48 * 1024 * 1024
        ),
    )(spectra, start, spread)


def solution(mesh):
    placed = (P("pix", "chan"), P(None, "chan"), P())
    return jax.shard_map(
        functools.partial(local, mesh.shape["pix"]),
        mesh=mesh,
        in_specs=placed,
        out_specs=(P(None, "pix"), P(None, "pix")),
        check_vma=False,
    )
```

time: 806 us -> 186 us (0.23)
  waiting for transfers between devices: 545 us -> 0 us
  Pallas kernels: 0 us -> 179 us
  blocking collectives: 107 us -> 0 us
  other arithmetic: 74.8 us -> 0 us
  matrix products: 60.1 us -> 0 us
  between operations: 14.2 us -> 0.64 us
    psum x11 -> x0, waiting for transfers between devices: 545 us -> none  [the longest x5 349 us: local(): full = lax.psum(back, 'pix')]
    pallas_call x0 -> x1, Pallas kernels: none -> 179 us  [local(): pl.pallas_call(functools.partial(kernel, n_pix), out_shape=(jax.ShapeDtyp...]
    psum x8 -> x0, blocking collectives: 107 us -> none  [the longest x5 51.3 us: local(): lax.psum(jnp.dot(full, full.T, precision=lax.Precision.HIGHEST), 'chan')]
    another operation x30 -> x0, other arithmetic: 64.4 us -> none  [the longest x15 32.6 us: local(): lower = jnp.linalg.cholesky(gram)]
    dot_general x19 -> x0, matrix products: 52.5 us -> none  [the longest x6 24 us: project(): lax.dot_general(loadings, weighted, (((1,), (1,)), ((), ())), preferred_e...]
  transfers between devices with their start and end apart: 11 -> 0, of which waited for: 11 -> 0; matrix products, arithmetic and copies ran while one was open for 0% -> 0% of each run, Pallas kernels for 0% -> 0%
where the time goes in v1:
time: 186 us; the launch traced here: 185 us
  Pallas kernels  179 us (96%)
  local copies, waits for them, and re-layouts  5.43 us (3%)
    pallas_call x1, Pallas kernels, local(): pl.pallas_call(functools.partial(kernel, n_pix), out_shape=(jax.ShapeDtyp...  179 us
    unnamed x6, local copies, waits for them, and re-layouts  4.7 us

profile of v1, /device:TPU:0, one launch (start us, length us, event | category | flops | bytes accessed | tf_op | source)
XLA Modules:
  0.0 185.4 jit_solution(16670432255493524441)
XLA Ops:
  0.6 0.7 broadcast_in_dim.2.anchors_ref
  1.4 0.0 copy-start
  1.4 2.2 %copy-done = bf16[4096,512]{1,0:T(8,128)(2,1)S(1)} copy-done((bf16[4096,512]{1,0:T(8,128)(2,1)S(1)}, bf16[4096,512]{1,0:T(8,128)(2,1)}, u32[]{:S(2)}) %copy-start) | copy-done | bytes 4194328
  3.5 0.0 copy-start.1
  3.5 0.8 copy-done.1
  4.4 179.4 %shard_map.50 = (f32[64,4096]{1,0:T(8,128)S(1)}, f32[16,4096]{1,0:T(8,128)S(1)}) custom-call(bf16[4096,512]{1,0:T(8,128)(2,1)S(1)} %copy-done, bf16[64,512]{1,0:T(8,128)(2,1)S(1)} %copy-done.1, s32[16,128]{1,0:T(8,128)S(1)} %broadcast_in_dim.2.anchors_ref), custom_call_target="tpu_custom_call" | custom-call | tf_op jit(solution)/shard_map/pallas_call | solution.py:316
  183.7 1.0 copy.7
  184.7 0.7 copy.8
Async XLA Ops:
  1.4 2.2 %copy-start = (bf16[4096,512]{1,0:T(8,128)(2,1)S(1)}, bf16[4096,512]{1,0:T(8,128)(2,1)}, u32[]{:S(2)}) copy-start(bf16[4096,512]{1,0:T(8,128)(2,1)} %s_ref.1) | copy-start | bytes 12582916
  3.5 0.8 copy-start.1

commit v2 on v1

--- a/solution.py
+++ b/solution.py
@@ -24,22 +24,33 @@
     n = gram.shape[0]
     rows = lax.broadcasted_iota(jnp.int32, (n, 128), 0)
     lanes = lax.broadcasted_iota(jnp.int32, (n, 128), 1)
-    full = jnp.where(lanes == rows, 1.0, gram)
+    full = jnp.where(lanes < 64, jnp.where(lanes == rows, 1.0, 0.0), gram)
     sub = lax.broadcasted_iota(jnp.int32, (8, 128), 0)
-    blocks = [full[8 * i : 8 * i + 8, :] for i in range(n // 8)]
-    for k in range(n):
-        home, r = k // 8, k % 8
-        row = blocks[home][r : r + 1, :]
-        scaled = row * (1.0 / row[:, 64 + k : 65 + k])
-        for i in range(home, n // 8):
-            column = blocks[i][:, 64 + k : 65 + k]
-            change = column * scaled
-            if i == home:
-                change = jnp.where(sub > r, change, 0.0)
-            blocks[i] = blocks[i] - change
-    full = jnp.concatenate(blocks, axis=0)
-    pivots = jnp.sum(jnp.where(lanes == rows + 64, full, 0.0), axis=1, keepdims=True)
-    return jnp.where(lanes < 64, full * lax.rsqrt(pivots), 0.0)
+    count = n // 8
+    blocks = [full[8 * i : 8 * i + 8, :] for i in range(count)]
+    done = []
+    for home in range(count):
+        spread = [
+            [jnp.broadcast_to(block[:, at : at + 1], (8, 128))
+             for at in range(64 + 8 * home, 72 + 8 * home)]
+            for block in blocks
+        ]
+        pivots = jnp.ones((8, 128), F32)
+        for r in range(8):
+            inverse = 1.0 / spread[0][r][r : r + 1, :]
+            pivots = jnp.where(sub == r, spread[0][r], pivots)
+            line = blocks[0][r : r + 1, :] * inverse
+            later = {c: spread[0][c][r : r + 1, :] * inverse for c in range(r + 1, 8)}
+            for i in range(len(blocks)):
+                ratio = spread[i][r]
+                if i == 0:
+                    ratio = jnp.where(sub > r, ratio, 0.0)
+                for c, value in later.items():
+                    spread[i][c] = spread[i][c] - ratio * value
+                blocks[i] = blocks[i] - ratio * line
+        done.append(blocks[0] * lax.rsqrt(pivots))
+        blocks = blocks[1:]
+    return jnp.where(lanes < 64, jnp.concatenate(done, axis=0), 0.0)
 
 
 def kernel(
@@ -228,7 +239,8 @@
         twin.start()
         back = ag[t]
         padded[k_rows : 2 * k_rows, :ch] = back
-        gram_out[t] = dot(back, padded[: 2 * k_rows, :ch], NT, HIGH)
+        gram_out[t] = dot(back[: k_rows // 2], padded[k_rows:, :ch], NT, HIGH) + dot(
+            back[k_rows // 2 :], padded[: 2 * k_rows, :ch], NT, HIGH)
         grams = [
             send(gram_out.at[t], gram_in.at[t, m], gram_sem.at[t, m], (pix, mates[m]))
             for m in range(3)
@@ -238,7 +250,7 @@
         for copy in grams:
             copy.wait()
         gram = (gram_out[t] + gram_in[t, 0]) + (gram_in[t, 1] + gram_in[t, 2])
-        factor = inverse_factor(gram)
+        factor = inverse_factor(jnp.concatenate([pltpu.roll(gram, 64, 1), gram], axis=0))
         twin.wait()
         padded[k_rows : 2 * k_rows, ch:] = back_in[t]
         load[...] = dot(factor, padded[k_rows:, :], precision=HIGH).astype(BF16)
@@ -306,7 +318,7 @@
         v((k, 2 * ch), F32), v((ITERS, k, ch), F32), v((ITERS, 2, k, ch), F32),
         v((ITERS, GROUP, k // GROUP, ch), F32), v((ITERS, n_hi, k // GROUP, ch), F32),
         v((ITERS, k, ch), F32), v((ITERS, k, ch), F32), v((3 * k, 2 * ch), F32),
-        v((ITERS, k, 2 * k), F32), v((ITERS, 3, k, 2 * k), F32),
+        v((ITERS, k // 2, 2 * k), F32), v((ITERS, 3, k // 2, 2 * k), F32),
         v((2 * chunks, k, step), F32), v((na, k), F32), v((na, k), F32), v((na, k), F32),
         v((n_pix, na, k), F32), v((192, k), F32),
         sem(), sem(), sem(n_pix), sem(3), sem(3), sem(ITERS + 1, chunks), sem(ITERS),

time: 186 us -> 166 us (0.89)
  Pallas kernels: 179 us -> 160 us
    pallas_call x1, Pallas kernels: 179 us -> 160 us  [local(): pl.pallas_call(functools.partial(kernel, n_pix), out_shape=(jax.ShapeDtyp...]
where the time goes in v2:
time: 166 us
  Pallas kernels  160 us (96%)
  local copies, waits for them, and re-layouts  5.43 us (3%)
    pallas_call x1, Pallas kernels, local(): pl.pallas_call(functools.partial(kernel, n_pix), out_shape=(jax.ShapeDtyp...  160 us
    unnamed x6, local copies, waits for them, and re-layouts  4.7 us

profile of v2, /device:TPU:0, one launch (start us, length us, event | category | flops | bytes accessed | tf_op | source)
XLA Modules:
  0.0 165.6 jit_solution(8897270361566402129)
XLA Ops:
  0.6 0.7 broadcast_in_dim.2.anchors_ref
  1.4 0.0 copy-start
  1.4 2.2 %copy-done = bf16[4096,512]{1,0:T(8,128)(2,1)S(1)} copy-done((bf16[4096,512]{1,0:T(8,128)(2,1)S(1)}, bf16[4096,512]{1,0:T(8,128)(2,1)}, u32[]{:S(2)}) %copy-start) | copy-done | bytes 4194328
  3.5 0.0 copy-start.1
  3.5 0.8 copy-done.1
  4.4 159.5 %shard_map.50 = (f32[64,4096]{1,0:T(8,128)S(1)}, f32[16,4096]{1,0:T(8,128)S(1)}) custom-call(bf16[4096,512]{1,0:T(8,128)(2,1)S(1)} %copy-done, bf16[64,512]{1,0:T(8,128)(2,1)S(1)} %copy-done.1, s32[16,128]{1,0:T(8,128)S(1)} %broadcast_in_dim.2.anchors_ref), custom_call_target="tpu_custom_call" | custom-call | tf_op jit(solution)/shard_map/pallas_call | solution.py:328
  163.9 1.0 copy.7
  164.9 0.7 copy.8
Async XLA Ops:
  1.4 2.2 %copy-start = (bf16[4096,512]{1,0:T(8,128)(2,1)S(1)}, bf16[4096,512]{1,0:T(8,128)(2,1)}, u32[]{:S(2)}) copy-start(bf16[4096,512]{1,0:T(8,128)(2,1)} %s_ref.1) | copy-start | bytes 12582916
  3.5 0.8 copy-start.1

commit v3 on v2

--- a/solution.py
+++ b/solution.py
@@ -53,12 +53,28 @@
     return jnp.where(lanes < 64, jnp.concatenate(done, axis=0), 0.0)
 
 
+def split_rows(ref, value, lanes):
+    top = value.astype(BF16)
+    n = value.shape[0]
+    ref[:n, lanes] = top
+    ref[n:, lanes] = (value - top.astype(F32)).astype(BF16)
+
+
+def split_dot(left, pair):
+    top = left.astype(BF16)
+    low = (left - top.astype(F32)).astype(BF16)
+    twice = (top.astype(F32) + pltpu.roll(top.astype(F32), 64, 1)).astype(BF16)
+    n = left.shape[0]
+    out = dot(jnp.concatenate([twice, low], axis=0), pair)
+    return out[:n] + out[n:]
+
+
 def kernel(
-    n_pix, s_ref, start_ref, anchors_ref, scores_ref, abund_ref,
-    other_s, start_in, col_out, col_in, col_mine, col_chan, row_out, row_in, row_sum,
+    n_pix, s_hbm, start_ref, anchors_ref, scores_ref, abund_ref,
+    s_ref, other_s, start_in, col_out, col_in, col_mine, col_chan, row_out, row_in, row_sum,
     w, wt, load, x_out, x_in, acc, half_in, keep, rs_in, hi_in, ag, back_in, padded,
     gram_out, gram_in, score, rows_half, rows_half_in, rows_out, rows_in, rows_pad,
-    s_sem, st_sem, col_sem, cc_sem, row_sem, x_sem, half_sem, rs_sem, hi_sem, ag_sem,
+    halves, pieces, in_sem, s_sem, st_sem, col_sem, cc_sem, row_sem, x_sem, half_sem, rs_sem, hi_sem, ag_sem,
     bk_sem, gram_sem, sc_sem, rh_sem, rows_sem,
 ):
     pix = lax.axis_index("pix")
@@ -86,6 +102,12 @@
             return carry
         lax.fori_loop(1, n_pix, body, 0)
 
+    loads = []
+    for j in range(2 * chunks):
+        part = pl.ds(j * step_pix, step_pix)
+        loads.append(pltpu.make_async_copy(s_hbm.at[part], s_ref.at[part], in_sem.at[j]))
+        loads[-1].start()
+
     barrier = pltpu.get_barrier_semaphore()
     for mate in mates:
         pl.semaphore_signal(barrier, inc=1, device_id=(pix, mate), device_id_type=MESH)
@@ -94,25 +116,31 @@
     pl.semaphore_wait(barrier, 3 + n_pix - 1)
 
     away = pl.multiple_of((1 - lo) * half, half)
-    swap = send(s_ref.at[pl.ds(away, half)], other_s, s_sem, (pix, mates[0]))
+    swap = send(s_hbm.at[pl.ds(away, half)], other_s, s_sem, (pix, mates[0]))
     swap.start()
     swap_start = send(start_ref, start_in, st_sem, (pix, mates[0]))
     swap_start.start()
 
-    ones = jnp.ones((8, step_pix), BF16)
     total_col = jnp.zeros((8, ch), F32)
     for j in range(2 * chunks):
-        total_col += dot(ones, s_ref[j * step_pix : (j + 1) * step_pix, :])
-    col_out[...] = total_col
+        loads[j].wait()
+        block = s_ref[j * step_pix : (j + 1) * step_pix, :].astype(F32)
+        total_col += jnp.sum(block.reshape(step_pix // 8, 8, ch), axis=0)
+    col_out[...] = jnp.sum(total_col, axis=0, keepdims=True)
 
     def col_copy(d, to):
         return send(col_out, col_in.at[d], col_sem.at[d], (to, chan))
     all_pix(lambda d, to: col_copy(d, to).start())
 
-    ones_ch = jnp.ones((8, ch), BF16)
-    for j in range(2 * chunks):
-        sums = dot(ones_ch, s_ref[j * step_pix : (j + 1) * step_pix, :], NT)
-        row_out[j : j + 1, :] = sums[0:1, :]
+    ones = jnp.ones((ch, 128), BF16)
+    diagonal = lax.broadcasted_iota(jnp.int32, (128, 128), 0) == (
+        lax.broadcasted_iota(jnp.int32, (128, 128), 1))
+    for j in range(2 * chunks):
+        sums = dot(s_ref[j * step_pix : (j + 1) * step_pix, :], ones)
+        for b in range(step_pix // 128):
+            square = jnp.where(diagonal, sums[b * 128 : (b + 1) * 128, :], 0.0)
+            row_out[j : j + 1, b * 128 : (b + 1) * 128] = jnp.sum(
+                square, axis=0, keepdims=True)
     row_copies = [
         send(row_out, row_in.at[m], row_sem.at[m], (pix, mates[m])) for m in range(3)
     ]
@@ -134,10 +162,10 @@
         row_sum[j] = jnp.broadcast_to(sums[j : j + 1, :], (8, step_pix))
     for copy in col_copies:
         copy.wait()
-    cols = (col_mine[0:1, :] + col_chan[0, 0:1, :]) + (
-        col_chan[1, 0:1, :] + col_chan[2, 0:1, :])
+    cols = (col_mine[...] + col_chan[0]) + (col_chan[1] + col_chan[2])
     inv_total = 1.0 / jnp.sum(cols, axis=1, keepdims=True)
-    shares = [col_mine[0:1, :] * inv_total, col_chan[0, 0:1, :] * inv_total]
+    shares = [col_mine[...] * inv_total, col_chan[0] * inv_total]
+    share_roots = [lax.rsqrt(share) for share in shares]
     swap.wait()
 
     tiles = step_pix // 128
@@ -147,16 +175,19 @@
         first = pl.multiple_of(q * 128, 128)
         line = row_sum[lo * chunks + j, 0:1, pl.ds(first, 128)]
         wide = jnp.transpose(jnp.broadcast_to(line, (128, 128)))
+        wide_root = lax.rsqrt(wide)
         mine = s_ref[pl.ds(pl.multiple_of(lo * half + i * 128, 128), 128), :]
         theirs = other_s[pl.ds(pl.multiple_of(i * 128, 128), 128), :]
         for side, counts in enumerate((mine, theirs)):
             for g in range(ch // 128):
-                expect = wide * shares[side][:, g * 128 : (g + 1) * 128]
-                value = counts[:, g * 128 : (g + 1) * 128].astype(F32)
-                weighted = (value - expect) * lax.rsqrt(expect)
+                lanes = slice(g * 128, (g + 1) * 128)
+                expect = wide * shares[side][:, lanes]
+                root = wide_root * share_roots[side][:, lanes]
+                value = counts[:, lanes].astype(F32)
+                weighted = ((value - expect) * root).astype(BF16)
                 at = side * ch + g * 128
-                w[j, pl.ds(first, 128), at : at + 128] = weighted.astype(BF16)
-                wt[j, at : at + 128, pl.ds(first, 128)] = jnp.transpose(weighted).astype(BF16)
+                w[j, pl.ds(first, 128), at : at + 128] = weighted
+                wt[j, at : at + 128, pl.ds(first, 128)] = jnp.transpose(weighted)
         return carry
     lax.fori_loop(0, chunks * tiles, weigh, 0)
 
@@ -238,9 +269,10 @@
         twin = send(ag.at[t], back_in.at[t], bk_sem.at[t], (pix, mates[0]))
         twin.start()
         back = ag[t]
-        padded[k_rows : 2 * k_rows, :ch] = back
-        gram_out[t] = dot(back[: k_rows // 2], padded[k_rows:, :ch], NT, HIGH) + dot(
-            back[k_rows // 2 :], padded[: 2 * k_rows, :ch], NT, HIGH)
+        padded[k_rows : 2 * k_rows, :] = back
+        split_rows(halves, back, slice(0, ch))
+        gram_out[t] = dot(back[: k_rows // 2], padded[k_rows:, :], NT, HIGH) + dot(
+            back[k_rows // 2 :], padded[: 2 * k_rows, :], NT, HIGH)
         grams = [
             send(gram_out.at[t], gram_in.at[t, m], gram_sem.at[t, m], (pix, mates[m]))
             for m in range(3)
@@ -252,14 +284,18 @@
         gram = (gram_out[t] + gram_in[t, 0]) + (gram_in[t, 1] + gram_in[t, 2])
         factor = inverse_factor(jnp.concatenate([pltpu.roll(gram, 64, 1), gram], axis=0))
         twin.wait()
-        padded[k_rows : 2 * k_rows, ch:] = back_in[t]
-        load[...] = dot(factor, padded[k_rows:, :], precision=HIGH).astype(BF16)
+        split_rows(halves, back_in[t], slice(ch, 2 * ch))
+        load[...] = split_dot(factor, halves[...]).astype(BF16)
         return carry
     lax.fori_loop(0, ITERS, iteration, 0)
 
     project(ITERS)
     n_anchor = anchors_ref.shape[0]
-    wanted = anchors_ref[...][:, :1] - pix * pixels - lo * half
+    order = lax.broadcasted_iota(jnp.int32, (n_anchor, step_pix), 0)
+    wanted = jnp.zeros((n_anchor, step_pix), jnp.int32)
+    for a in range(n_anchor):
+        wanted = jnp.where(order == a, anchors_ref[a], wanted)
+    wanted = wanted - pix * pixels - lo * half
     rows_half[...] = jnp.zeros_like(rows_half)
 
     def finish(j, carry):
@@ -285,16 +321,17 @@
         slot = lo * chunks + j
         send(score.at[slot], score.at[slot], sc_sem.at[j], (pix, mates[0])).wait()
     for j in range(2 * chunks):
-        scores_ref[:, j * step_pix : (j + 1) * step_pix] = score[j]
+        part = slice(j * step_pix, (j + 1) * step_pix)
+        scores_ref[:, part] = score[j]
+        split_rows(pieces, score[j], part)
     all_pix(lambda d, to: rows_copy(d, to).wait())
     rows = jnp.sum(rows_in[...], axis=0)
-    rows_pad[64 : 64 + n_anchor, :] = rows
-    small = dot(rows, rows_pad[0:128, :], NT, HIGH)
+    rows_pad[64 : 64 + n_anchor, :k_rows] = rows
+    small = dot(rows_pad[64 : 64 + n_anchor, :], rows_pad[0:128, :], NT, HIGH)
     factor = inverse_factor(small)
     solved = dot(factor, rows_pad[64:192, :], precision=HIGH)
     both = dot(jnp.transpose(factor)[:n_anchor, :], solved, precision=HIGH)
-    for j in range(2 * chunks):
-        abund_ref[:, j * step_pix : (j + 1) * step_pix] = dot(both, score[j], precision=HIGH)
+    abund_ref[...] = split_dot(both, pieces[...])
 
 
 def local(n_pix, spectra, start, anchors):
@@ -305,23 +342,25 @@
     step = min(512, half)
     chunks = half // step
     n_hi = n_pix // GROUP
-    spread = jnp.broadcast_to(anchors[:, None], (na, 128))
     vmem = pl.BlockSpec(memory_space=pltpu.VMEM)
+    smem = pl.BlockSpec(memory_space=pltpu.SMEM)
+    hbm = pl.BlockSpec(memory_space=pl.ANY)
     v = pltpu.VMEM
     sem = lambda *shape: pltpu.SemaphoreType.DMA(tuple(shape) + (2,))
     scratch = [
-        v((half, ch), BF16), v((k, ch), BF16), v((8, ch), F32), v((n_pix, 8, ch), F32),
-        v((8, ch), F32), v((3, 8, ch), F32), v((2 * chunks, step), F32),
+        v((pixels, ch), BF16), v((half, ch), BF16), v((k, ch), BF16), v((1, ch), F32),
+        v((n_pix, 1, ch), F32), v((1, ch), F32), v((3, 1, ch), F32), v((2 * chunks, step), F32),
         v((3, 2 * chunks, step), F32), v((2 * chunks, 8, step), F32),
         v((chunks, step, 2 * ch), BF16), v((chunks, 2 * ch, step), BF16), v((k, 2 * ch), BF16),
         v((ITERS + 1, chunks, k, step), BF16), v((ITERS + 1, chunks, k, step), BF16),
         v((k, 2 * ch), F32), v((ITERS, k, ch), F32), v((ITERS, 2, k, ch), F32),
         v((ITERS, GROUP, k // GROUP, ch), F32), v((ITERS, n_hi, k // GROUP, ch), F32),
-        v((ITERS, k, ch), F32), v((ITERS, k, ch), F32), v((3 * k, 2 * ch), F32),
+        v((ITERS, k, ch), F32), v((ITERS, k, ch), F32), v((3 * k, ch), F32),
         v((ITERS, k // 2, 2 * k), F32), v((ITERS, 3, k // 2, 2 * k), F32),
         v((2 * chunks, k, step), F32), v((na, k), F32), v((na, k), F32), v((na, k), F32),
-        v((n_pix, na, k), F32), v((192, k), F32),
-        sem(), sem(), sem(n_pix), sem(3), sem(3), sem(ITERS + 1, chunks), sem(ITERS),
+        v((n_pix, na, k), F32), v((192, 128), F32),
+        v((2 * k, 2 * ch), BF16), v((2 * k, pixels), BF16),
+        pltpu.SemaphoreType.DMA((2 * chunks,)), sem(), sem(), sem(n_pix), sem(3), sem(3), sem(ITERS + 1, chunks), sem(ITERS),
         sem(ITERS, GROUP), sem(ITERS, n_hi), sem(ITERS, GROUP), sem(ITERS), sem(ITERS, 3),
         sem(chunks), sem(), sem(n_pix),
     ]
@@ -331,13 +370,13 @@
             jax.ShapeDtypeStruct((k, pixels), F32),
             jax.ShapeDtypeStruct((na, pixels), F32),
         ),
-        in_specs=[vmem] * 3,
+        in_specs=[hbm, vmem, smem],
         out_specs=(vmem, vmem),
         scratch_shapes=scratch,
         compiler_params=pltpu.CompilerParams(
-            collective_id=0, has_side_effects=True, vmem_limit_bytes=48 * 1024 * 1024
+            collective_id=0, has_side_effects=True, vmem_limit_bytes=60 * 1024 * 1024
         ),
-    )(spectra, start, spread)
+    )(spectra, start, anchors)
 
 
 def solution(mesh):

time: 166 us -> 163 us (0.982)
  Pallas kernels: 160 us -> 158 us
    pallas_call x1, Pallas kernels: 160 us -> 158 us  [local(): pl.pallas_call(functools.partial(kernel, n_pix), out_shape=(jax.ShapeDtyp...]
    unnamed x6 -> x2, local copies, waits for them, and re-layouts: 4.7 us -> 3.94 us
where the time goes in v3:
time: 163 us; the launch traced here: 162 us
  Pallas kernels  158 us (97%)
  local copies, waits for them, and re-layouts  3.94 us (2%)
    pallas_call x1, Pallas kernels, local(): pl.pallas_call(functools.partial(kernel, n_pix), out_shape=(jax.ShapeDtyp...  158 us
    unnamed x2, local copies, waits for them, and re-layouts  3.94 us

profile of v3, /device:TPU:0, one launch (start us, length us, event | category | flops | bytes accessed | tf_op | source)
XLA Modules:
  0.0 162.4 jit_solution(6576228307326858267)
XLA Ops:
  0.6 157.8 %shard_map.50 = (f32[64,4096]{1,0:T(8,128)}, f32[16,4096]{1,0:T(8,128)}) custom-call(bf16[4096,512]{1,0:T(8,128)(2,1)} %s_hbm.1, bf16[64,512]{1,0:T(8,128)(2,1)} %start_ref.1, s32[16]{0:T(128)} %anchors_ref.1), custom_call_target="tpu_custom_call" | custom-call | tf_op jit(solution)/shard_map/pallas_call | solution.py:367
  158.5 2.3 %copy.7 = f32[64,4096]{1,0:T(8,128)} copy(f32[64,4096]{1,0:T(8,128)} %get-tuple-element.4) | data formatting | bytes 2097152
  160.7 1.7 %copy.8 = f32[16,4096]{1,0:T(8,128)} copy(f32[16,4096]{1,0:T(8,128)} %get-tuple-element.5) | data formatting | bytes 524288

commit v4 on v3

--- a/solution.py
+++ b/solution.py
@@ -72,9 +72,9 @@
 def kernel(
     n_pix, s_hbm, start_ref, anchors_ref, scores_ref, abund_ref,
     s_ref, other_s, start_in, col_out, col_in, col_mine, col_chan, row_out, row_in, row_sum,
-    w, wt, load, x_out, x_in, acc, half_in, keep, rs_in, hi_in, ag, back_in, padded,
+    w, wt, load, x_out, x_in, acc, mate_out, half_in, keep, rs_in, hi_in, ag, back_in, padded,
     gram_out, gram_in, score, rows_half, rows_half_in, rows_out, rows_in, rows_pad,
-    halves, pieces, in_sem, s_sem, st_sem, col_sem, cc_sem, row_sem, x_sem, half_sem, rs_sem, hi_sem, ag_sem,
+    halves, theirs, pieces, in_sem, s_sem, st_sem, col_sem, cc_sem, row_sem, x_sem, half_sem, rs_sem, hi_sem, ag_sem,
     bk_sem, gram_sem, sc_sem, rh_sem, rows_sem,
 ):
     pix = lax.axis_index("pix")
@@ -115,11 +115,16 @@
         barrier, inc=1, device_id=(to, chan), device_id_type=MESH))
     pl.semaphore_wait(barrier, 3 + n_pix - 1)
 
-    away = pl.multiple_of((1 - lo) * half, half)
-    swap = send(s_hbm.at[pl.ds(away, half)], other_s, s_sem, (pix, mates[0]))
-    swap.start()
+    def swap_copy(j):
+        away = pl.multiple_of(((1 - lo) * chunks + j) * step_pix, step_pix)
+        return send(
+            s_hbm.at[pl.ds(away, step_pix)],
+            other_s.at[pl.ds(pl.multiple_of(j * step_pix, step_pix), step_pix)],
+            s_sem.at[j], (pix, mates[0]))
     swap_start = send(start_ref, start_in, st_sem, (pix, mates[0]))
     swap_start.start()
+    for j in range(chunks):
+        swap_copy(j).start()
 
     total_col = jnp.zeros((8, ch), F32)
     for j in range(2 * chunks):
@@ -166,12 +171,46 @@
     inv_total = 1.0 / jnp.sum(cols, axis=1, keepdims=True)
     shares = [col_mine[...] * inv_total, col_chan[0] * inv_total]
     share_roots = [lax.rsqrt(share) for share in shares]
-    swap.wait()
 
     tiles = step_pix // 128
 
-    def weigh(i, carry):
-        j, q = lax.div(i, tiles), lax.rem(i, tiles)
+    swap_start.wait()
+    load[:, :ch] = start_ref[...]
+    load[:, ch:] = start_in[...]
+    padded[...] = jnp.zeros_like(padded)
+    rows_pad[...] = jnp.zeros_like(rows_pad)
+
+    rows_part = k_rows // 2
+    slab_lanes = ch * rows_part // (8 * GROUP)
+    across = ch // slab_lanes
+
+    def x_copy(t, h, j):
+        return send(
+            x_out.at[t, h, j], x_in.at[t, h, j], x_sem.at[t, h, j], (pix, mates[1]))
+
+    def project_chunk(t, j):
+        part = dot(load[...], wt[j]).astype(BF16)
+        x_out[t, 0, j] = part[:rows_part]
+        x_out[t, 1, j] = part[rows_part:]
+        x_copy(t, 0, j).start()
+
+    def later_half(t):
+        for j in range(chunks):
+            x_copy(t, 1, j).start()
+
+    def project(t):
+        def body(j, carry):
+            project_chunk(t, j)
+            return carry
+        lax.fori_loop(0, chunks, body, 0)
+        later_half(t)
+
+    def gather(t, h, j):
+        x_copy(t, h, j).wait()
+        return x_out[t, h, j].astype(F32) + x_in[t, h, j].astype(F32)
+
+    def weigh(j, q):
+        i = j * tiles + q
         first = pl.multiple_of(q * 128, 128)
         line = row_sum[lo * chunks + j, 0:1, pl.ds(first, 128)]
         wide = jnp.transpose(jnp.broadcast_to(line, (128, 128)))
@@ -188,108 +227,138 @@
                 at = side * ch + g * 128
                 w[j, pl.ds(first, 128), at : at + 128] = weighted
                 wt[j, at : at + 128, pl.ds(first, 128)] = jnp.transpose(weighted)
+
+    def opening(j, carry):
+        swap_copy(j).wait()
+
+        def tile(q, inner):
+            weigh(j, q)
+            return inner
+        lax.fori_loop(0, tiles, tile, 0)
+        project_chunk(0, j)
         return carry
-    lax.fori_loop(0, chunks * tiles, weigh, 0)
-
-    swap_start.wait()
-    load[:, :ch] = start_ref[...]
-    load[:, ch:] = start_in[...]
-    padded[...] = jnp.zeros_like(padded)
-    rows_pad[...] = jnp.zeros_like(rows_pad)
-
-    def x_copy(t, j):
-        return send(x_out.at[t, j], x_in.at[t, j], x_sem.at[t, j], (pix, mates[1]))
-
-    def project(t):
+    lax.fori_loop(0, chunks, opening, 0)
+    later_half(0)
+
+    def slab_at(i):
+        return slice(8 * (i // across), 8 * (i // across) + 8), (i % across) * slab_lanes
+
+    def accumulate(t, h, first, last):
         def body(j, carry):
-            x_out[t, j] = dot(load[...], wt[j]).astype(BF16)
-            x_copy(t, j).start()
+            acc[...] += dot(gather(t, h, j).astype(BF16), w[j])
             return carry
-        lax.fori_loop(0, chunks, body, 0)
-
-    def gather(t, j):
-        x_copy(t, j).wait()
-        return x_out[t, j].astype(F32) + x_in[t, j].astype(F32)
-
-    per = k_rows // GROUP
-
-    def iteration(t, carry):
-        project(t)
+        lax.fori_loop(first, last, body, 0)
+
+    def pair_copy(t, h):
+        return send(
+            mate_out.at[t, h], half_in.at[t, h], half_sem.at[t, h], (pix, mates[0]))
+
+    def pair_start(t, h):
+        for i in range(GROUP):
+            rows, at = slab_at(i)
+            mate_out[t, h, i] = acc[rows, ch + at : ch + at + slab_lanes]
+            keep[t, h, i] = acc[rows, at : at + slab_lanes]
+        pair_copy(t, h).start()
         acc[...] = jnp.zeros_like(acc)
 
-        def body(j, carry):
-            acc[...] += dot(gather(t, j).astype(BF16), w[j])
-            return carry
-        lax.fori_loop(0, chunks, body, 0)
-
-        keep[t, 0] = acc[:, ch:]
-        copy = send(keep.at[t, 0], half_in.at[t], half_sem.at[t], (pix, mates[0]))
-        copy.start()
-        copy.wait()
-        keep[t, 1] = acc[:, :ch] + half_in[t]
-
-        def partner(d):
-            return lax.rem(low + d, GROUP)
-        spread = [
-            send(
-                keep.at[t, 1, pl.ds(pl.multiple_of(partner(d) * per, per), per)],
-                rs_in.at[t, d], rs_sem.at[t, d], (base + partner(d), chan))
+    def partner(d):
+        return lax.rem(low + d, GROUP)
+
+    def scatter_copies(t, h):
+        return [
+            send(keep.at[t, h, partner(d)], rs_in.at[t, h, d], rs_sem.at[t, h, d],
+                 (base + partner(d), chan))
             for d in range(1, GROUP)
         ]
-        for copy in spread:
+
+    def pair_finish(t, h):
+        pair_copy(t, h).wait()
+        keep[t, h] = keep[t, h] + half_in[t, h]
+        for copy in scatter_copies(t, h):
             copy.start()
-        slab = keep[t, 1, pl.ds(pl.multiple_of(low * per, per), per), :]
-        for d, copy in enumerate(spread, 1):
+
+    def collect_copies(t, h):
+        return [
+            send(ag.at[t, h, low], ag.at[t, h, low], ag_sem.at[t, h, d],
+                 (base + partner(d), chan))
+            for d in range(1, GROUP)
+        ]
+
+    def scatter_finish(t, h):
+        slab = keep[t, h, low]
+        for d, copy in enumerate(scatter_copies(t, h), 1):
             copy.wait()
-            slab = slab + rs_in[t, d]
+            slab = slab + rs_in[t, h, d]
         if n_hi > 1:
-            hi_in[t, 0] = slab
-            across = [
-                send(hi_in.at[t, 0], hi_in.at[t, e], hi_sem.at[t, e],
+            hi_in[t, h, 0] = slab
+            groups = [
+                send(hi_in.at[t, h, 0], hi_in.at[t, h, e], hi_sem.at[t, h, e],
                      (lax.rem(pix + e * GROUP, n_pix), chan))
                 for e in range(1, n_hi)
             ]
-            for copy in across:
+            for copy in groups:
                 copy.start()
-            for copy in across:
+            for copy in groups:
                 copy.wait()
-            slab = hi_in[t, lax.rem(n_hi + lax.div(pix, GROUP), n_hi)]
+            place = lax.div(pix, GROUP)
+            slab = hi_in[t, h, lax.rem(n_hi + place, n_hi)]
             for e in range(1, n_hi):
-                slab = slab + hi_in[t, lax.rem(n_hi + lax.div(pix, GROUP) - e, n_hi)]
-        mine = pl.ds(pl.multiple_of(low * per, per), per)
-        ag[t, mine] = slab
-        collect = [
-            send(ag.at[t, mine], ag.at[t, mine], ag_sem.at[t, d], (base + partner(d), chan))
-            for d in range(1, GROUP)
-        ]
-        for copy in collect:
+                slab = slab + hi_in[t, h, lax.rem(n_hi + place - e, n_hi)]
+        ag[t, h, low] = slab
+        for copy in collect_copies(t, h):
             copy.start()
-        for copy in collect:
+
+    def twin_copy(t, h):
+        return send(ag.at[t, h], back_in.at[t, h], bk_sem.at[t, h], (pix, mates[0]))
+
+    def collect_finish(t, h):
+        for copy in collect_copies(t, h):
             copy.wait()
-        twin = send(ag.at[t], back_in.at[t], bk_sem.at[t], (pix, mates[0]))
-        twin.start()
-        back = ag[t]
-        padded[k_rows : 2 * k_rows, :] = back
-        split_rows(halves, back, slice(0, ch))
-        gram_out[t] = dot(back[: k_rows // 2], padded[k_rows:, :], NT, HIGH) + dot(
-            back[k_rows // 2 :], padded[: 2 * k_rows, :], NT, HIGH)
+        twin_copy(t, h).start()
+        for i in range(GROUP):
+            rows, at = slab_at(i)
+            first = k_rows + h * rows_part + rows.start
+            padded[first : first + 8, at : at + slab_lanes] = ag[t, h, i]
+
+    def iteration(t, carry):
+        accumulate(t, 0, 0, chunks)
+        pair_start(t, 0)
+        accumulate(t, 1, 0, chunks // 2)
+        pair_finish(t, 0)
+        accumulate(t, 1, chunks // 2, chunks)
+        pair_start(t, 1)
+        scatter_finish(t, 0)
+        pair_finish(t, 1)
+        collect_finish(t, 0)
+        scatter_finish(t, 1)
+        collect_finish(t, 1)
+        back = padded[k_rows : 2 * k_rows, :]
+        gram_out[t] = dot(back[:rows_part], padded[k_rows:, :], NT, HIGH) + dot(
+            back[rows_part:], padded[: 2 * k_rows, :], NT, HIGH)
         grams = [
             send(gram_out.at[t], gram_in.at[t, m], gram_sem.at[t, m], (pix, mates[m]))
             for m in range(3)
         ]
         for copy in grams:
             copy.start()
+        split_rows(halves, back, slice(0, ch))
+        for h in range(2):
+            twin_copy(t, h).wait()
+            for i in range(GROUP):
+                rows, at = slab_at(i)
+                first = h * rows_part + rows.start
+                theirs[first : first + 8, at : at + slab_lanes] = back_in[t, h, i]
+        split_rows(halves, theirs[...], slice(ch, 2 * ch))
         for copy in grams:
             copy.wait()
         gram = (gram_out[t] + gram_in[t, 0]) + (gram_in[t, 1] + gram_in[t, 2])
         factor = inverse_factor(jnp.concatenate([pltpu.roll(gram, 64, 1), gram], axis=0))
-        twin.wait()
-        split_rows(halves, back_in[t], slice(ch, 2 * ch))
         load[...] = split_dot(factor, halves[...]).astype(BF16)
+        project(t + 1)
         return carry
+    acc[...] = jnp.zeros_like(acc)
     lax.fori_loop(0, ITERS, iteration, 0)
 
-    project(ITERS)
     n_anchor = anchors_ref.shape[0]
     order = lax.broadcasted_iota(jnp.int32, (n_anchor, step_pix), 0)
     wanted = jnp.zeros((n_anchor, step_pix), jnp.int32)
@@ -299,7 +368,7 @@
     rows_half[...] = jnp.zeros_like(rows_half)
 
     def finish(j, carry):
-        value = gather(ITERS, j)
+        value = jnp.concatenate([gather(ITERS, 0, j), gather(ITERS, 1, j)], axis=0)
         slot = lo * chunks + j
         score[slot] = value
         send(score.at[slot], score.at[slot], sc_sem.at[j], (pix, mates[0])).start()
@@ -344,24 +413,26 @@
     n_hi = n_pix // GROUP
     vmem = pl.BlockSpec(memory_space=pltpu.VMEM)
     smem = pl.BlockSpec(memory_space=pltpu.SMEM)
-    hbm = pl.BlockSpec(memory_space=pl.ANY)
+    hbm = pl.BlockSpec(memory_space=pltpu.HBM)
     v = pltpu.VMEM
     sem = lambda *shape: pltpu.SemaphoreType.DMA(tuple(shape) + (2,))
+    slabs = lambda count: v((ITERS, 2, count, 8, ch * (k // 2) // (8 * GROUP)), F32)
     scratch = [
         v((pixels, ch), BF16), v((half, ch), BF16), v((k, ch), BF16), v((1, ch), F32),
         v((n_pix, 1, ch), F32), v((1, ch), F32), v((3, 1, ch), F32), v((2 * chunks, step), F32),
         v((3, 2 * chunks, step), F32), v((2 * chunks, 8, step), F32),
         v((chunks, step, 2 * ch), BF16), v((chunks, 2 * ch, step), BF16), v((k, 2 * ch), BF16),
-        v((ITERS + 1, chunks, k, step), BF16), v((ITERS + 1, chunks, k, step), BF16),
-        v((k, 2 * ch), F32), v((ITERS, k, ch), F32), v((ITERS, 2, k, ch), F32),
-        v((ITERS, GROUP, k // GROUP, ch), F32), v((ITERS, n_hi, k // GROUP, ch), F32),
-        v((ITERS, k, ch), F32), v((ITERS, k, ch), F32), v((3 * k, ch), F32),
+        v((ITERS + 1, 2, chunks, k // 2, step), BF16),
+        v((ITERS + 1, 2, chunks, k // 2, step), BF16),
+        v((k // 2, 2 * ch), F32), slabs(GROUP), slabs(GROUP), slabs(GROUP), slabs(GROUP),
+        slabs(n_hi), slabs(GROUP), slabs(GROUP), v((3 * k, ch), F32),
         v((ITERS, k // 2, 2 * k), F32), v((ITERS, 3, k // 2, 2 * k), F32),
         v((2 * chunks, k, step), F32), v((na, k), F32), v((na, k), F32), v((na, k), F32),
         v((n_pix, na, k), F32), v((192, 128), F32),
-        v((2 * k, 2 * ch), BF16), v((2 * k, pixels), BF16),
-        pltpu.SemaphoreType.DMA((2 * chunks,)), sem(), sem(), sem(n_pix), sem(3), sem(3), sem(ITERS + 1, chunks), sem(ITERS),
-        sem(ITERS, GROUP), sem(ITERS, n_hi), sem(ITERS, GROUP), sem(ITERS), sem(ITERS, 3),
+        v((2 * k, 2 * ch), BF16), v((k, ch), F32), v((2 * k, pixels), BF16),
+        pltpu.SemaphoreType.DMA((2 * chunks,)), sem(chunks), sem(), sem(n_pix), sem(3), sem(3), sem(ITERS + 1, 2, chunks),
+        sem(ITERS, 2), sem(ITERS, 2, GROUP), sem(ITERS, 2, n_hi), sem(ITERS, 2, GROUP),
+        sem(ITERS, 2), sem(ITERS, 3),
         sem(chunks), sem(), sem(n_pix),
     ]
     return pl.pallas_call(
@@ -374,7 +445,7 @@
         out_specs=(vmem, vmem),
         scratch_shapes=scratch,
         compiler_params=pltpu.CompilerParams(
-            collective_id=0, has_side_effects=True, vmem_limit_bytes=60 * 1024 * 1024
+            collective_id=0, has_side_effects=True, vmem_limit_bytes=36 * 1024 * 1024
         ),
     )(spectra, start, anchors)
 

time: 163 us -> 171 us (1.049)
  Pallas kernels: 158 us -> 165 us
    pallas_call x1, Pallas kernels: 158 us -> 165 us  [local(): pl.pallas_call(functools.partial(kernel, n_pix), out_shape=(jax.ShapeDtyp...]
    unnamed x2 -> x8, local copies, waits for them, and re-layouts: 3.94 us -> 5.35 us
where the time goes in v4:
time: 171 us
  Pallas kernels  165 us (96%)
  local copies, waits for them, and re-layouts  5.35 us (3%)
    pallas_call x1, Pallas kernels, local(): pl.pallas_call(functools.partial(kernel, n_pix), out_shape=(jax.ShapeDtyp...  165 us
    unnamed x8, local copies, waits for them, and re-layouts  5.35 us

profile of v4, /device:TPU:0, one launch (start us, length us, event | category | flops | bytes accessed | tf_op | source)
XLA Modules:
  0.0 170.5 jit_solution(13320696889163417991)
XLA Ops:
  0.6 0.0 copy-start
  0.6 2.2 %copy-done = bf16[4096,512]{1,0:T(8,128)(2,1)S(1)} copy-done((bf16[4096,512]{1,0:T(8,128)(2,1)S(1)}, bf16[4096,512]{1,0:T(8,128)(2,1)}, u32[]{:S(2)}) %copy-start) | copy-done | bytes 4194328
  2.8 0.0 copy-start.1
  2.8 0.8 copy-done.1
  3.7 0.0 copy-start.2
  3.7 0.7 copy-done.2
  4.3 164.5 %shard_map.50 = (f32[64,4096]{1,0:T(8,128)S(1)}, f32[16,4096]{1,0:T(8,128)S(1)}) custom-call(bf16[4096,512]{1,0:T(8,128)(2,1)S(1)} %copy-done, bf16[64,512]{1,0:T(8,128)(2,1)S(1)} %copy-done.1, s32[16]{0:T(128)S(1)} %copy-done.2), custom_call_target="tpu_custom_call" | custom-call | tf_op jit(solution)/shard_map/pallas_call | solution.py:438
  168.8 1.0 copy.7
  169.8 0.7 copy.8
Async XLA Ops:
  0.6 2.2 %copy-start = (bf16[4096,512]{1,0:T(8,128)(2,1)S(1)}, bf16[4096,512]{1,0:T(8,128)(2,1)}, u32[]{:S(2)}) copy-start(bf16[4096,512]{1,0:T(8,128)(2,1)} %s_hbm.1) | copy-start | bytes 12582916
  2.8 0.8 copy-start.1
  3.7 0.7 copy-start.2

commit v5 on v3

--- a/solution.py
+++ b/solution.py
@@ -8,6 +8,7 @@
 from jax.sharding import PartitionSpec as P
 
 ITERS = 5
+FIRST_LATE = 2
 GROUP = 8
 MESH = pl.DeviceIdType.MESH
 HIGH = lax.Precision.HIGHEST
@@ -74,7 +75,7 @@
     s_ref, other_s, start_in, col_out, col_in, col_mine, col_chan, row_out, row_in, row_sum,
     w, wt, load, x_out, x_in, acc, half_in, keep, rs_in, hi_in, ag, back_in, padded,
     gram_out, gram_in, score, rows_half, rows_half_in, rows_out, rows_in, rows_pad,
-    halves, pieces, in_sem, s_sem, st_sem, col_sem, cc_sem, row_sem, x_sem, half_sem, rs_sem, hi_sem, ag_sem,
+    halves, shares_split, factor_ref, pieces, in_sem, s_sem, st_sem, col_sem, cc_sem, row_sem, x_sem, half_sem, rs_sem, hi_sem, ag_sem,
     bk_sem, gram_sem, sc_sem, rh_sem, rows_sem,
 ):
     pix = lax.axis_index("pix")
@@ -115,11 +116,16 @@
         barrier, inc=1, device_id=(to, chan), device_id_type=MESH))
     pl.semaphore_wait(barrier, 3 + n_pix - 1)
 
-    away = pl.multiple_of((1 - lo) * half, half)
-    swap = send(s_hbm.at[pl.ds(away, half)], other_s, s_sem, (pix, mates[0]))
-    swap.start()
+    def swap_copy(j):
+        away = pl.multiple_of(((1 - lo) * chunks + j) * step_pix, step_pix)
+        return send(
+            s_hbm.at[pl.ds(away, step_pix)],
+            other_s.at[pl.ds(pl.multiple_of(j * step_pix, step_pix), step_pix)],
+            s_sem.at[j], (pix, mates[0]))
     swap_start = send(start_ref, start_in, st_sem, (pix, mates[0]))
     swap_start.start()
+    for j in range(chunks):
+        swap_copy(j).start()
 
     total_col = jnp.zeros((8, ch), F32)
     for j in range(2 * chunks):
@@ -166,12 +172,38 @@
     inv_total = 1.0 / jnp.sum(cols, axis=1, keepdims=True)
     shares = [col_mine[...] * inv_total, col_chan[0] * inv_total]
     share_roots = [lax.rsqrt(share) for share in shares]
-    swap.wait()
 
     tiles = step_pix // 128
 
-    def weigh(i, carry):
-        j, q = lax.div(i, tiles), lax.rem(i, tiles)
+    swap_start.wait()
+    load[:, :ch] = start_ref[...]
+    load[:, ch:] = start_in[...]
+    padded[...] = jnp.zeros_like(padded)
+    rows_pad[...] = jnp.zeros_like(rows_pad)
+
+    def x_copy(t, j):
+        return send(x_out.at[t, j], x_in.at[t, j], x_sem.at[t, j], (pix, mates[1]))
+
+    def project_chunk(t, j):
+        x_out[t, j] = dot(load[...], wt[j]).astype(BF16)
+        x_copy(t, j).start()
+
+    def project(t):
+        def body(j, carry):
+            project_chunk(t, j)
+            return carry
+        lax.fori_loop(0, chunks, body, 0)
+
+    def gather(t, j):
+        x_copy(t, j).wait()
+        return x_out[t, j].astype(F32) + x_in[t, j].astype(F32)
+
+    def normal(value):
+        split_rows(shares_split, value, slice(0, step_pix))
+        return split_dot(factor_ref[...], shares_split[...])
+
+    def weigh(j, q):
+        i = j * tiles + q
         first = pl.multiple_of(q * 128, 128)
         line = row_sum[lo * chunks + j, 0:1, pl.ds(first, 128)]
         wide = jnp.transpose(jnp.broadcast_to(line, (128, 128)))
@@ -188,37 +220,28 @@
                 at = side * ch + g * 128
                 w[j, pl.ds(first, 128), at : at + 128] = weighted
                 wt[j, at : at + 128, pl.ds(first, 128)] = jnp.transpose(weighted)
+
+    def opening(j, carry):
+        swap_copy(j).wait()
+
+        def tile(q, inner):
+            weigh(j, q)
+            return inner
+        lax.fori_loop(0, tiles, tile, 0)
+        project_chunk(0, j)
         return carry
-    lax.fori_loop(0, chunks * tiles, weigh, 0)
-
-    swap_start.wait()
-    load[:, :ch] = start_ref[...]
-    load[:, ch:] = start_in[...]
-    padded[...] = jnp.zeros_like(padded)
-    rows_pad[...] = jnp.zeros_like(rows_pad)
-
-    def x_copy(t, j):
-        return send(x_out.at[t, j], x_in.at[t, j], x_sem.at[t, j], (pix, mates[1]))
-
-    def project(t):
+    lax.fori_loop(0, chunks, opening, 0)
+
+    per = k_rows // GROUP
+
+    def iteration(late, defer, t, carry):
+        acc[...] = jnp.zeros_like(acc)
+
         def body(j, carry):
-            x_out[t, j] = dot(load[...], wt[j]).astype(BF16)
-            x_copy(t, j).start()
-            return carry
-        lax.fori_loop(0, chunks, body, 0)
-
-    def gather(t, j):
-        x_copy(t, j).wait()
-        return x_out[t, j].astype(F32) + x_in[t, j].astype(F32)
-
-    per = k_rows // GROUP
-
-    def iteration(t, carry):
-        project(t)
-        acc[...] = jnp.zeros_like(acc)
-
-        def body(j, carry):
-            acc[...] += dot(gather(t, j).astype(BF16), w[j])
+            value = gather(t, j)
+            if late:
+                value = normal(value)
+            acc[...] += dot(value.astype(BF16), w[j])
             return carry
         lax.fori_loop(0, chunks, body, 0)
 
@@ -270,7 +293,6 @@
         twin.start()
         back = ag[t]
         padded[k_rows : 2 * k_rows, :] = back
-        split_rows(halves, back, slice(0, ch))
         gram_out[t] = dot(back[: k_rows // 2], padded[k_rows:, :], NT, HIGH) + dot(
             back[k_rows // 2 :], padded[: 2 * k_rows, :], NT, HIGH)
         grams = [
@@ -279,17 +301,34 @@
         ]
         for copy in grams:
             copy.start()
-        for copy in grams:
-            copy.wait()
-        gram = (gram_out[t] + gram_in[t, 0]) + (gram_in[t, 1] + gram_in[t, 2])
-        factor = inverse_factor(jnp.concatenate([pltpu.roll(gram, 64, 1), gram], axis=0))
-        twin.wait()
-        split_rows(halves, back_in[t], slice(ch, 2 * ch))
-        load[...] = split_dot(factor, halves[...]).astype(BF16)
+        def factor_of():
+            for copy in grams:
+                copy.wait()
+            gram = (gram_out[t] + gram_in[t, 0]) + (gram_in[t, 1] + gram_in[t, 2])
+            return inverse_factor(
+                jnp.concatenate([pltpu.roll(gram, 64, 1), gram], axis=0))
+
+        if defer:
+            load[:, :ch] = back.astype(BF16)
+            twin.wait()
+            load[:, ch:] = back_in[t].astype(BF16)
+            project(t + 1)
+            factor_ref[...] = factor_of()
+        else:
+            split_rows(halves, back, slice(0, ch))
+            factor = factor_of()
+            twin.wait()
+            split_rows(halves, back_in[t], slice(ch, 2 * ch))
+            load[...] = split_dot(factor, halves[...]).astype(BF16)
+            project(t + 1)
         return carry
-    lax.fori_loop(0, ITERS, iteration, 0)
-
-    project(ITERS)
+    plain = functools.partial(iteration, False, False)
+    first = functools.partial(iteration, False, True)
+    later = functools.partial(iteration, True, True)
+    lax.fori_loop(0, FIRST_LATE, plain, 0)
+    first(FIRST_LATE, 0)
+    lax.fori_loop(FIRST_LATE + 1, ITERS, later, 0)
+
     n_anchor = anchors_ref.shape[0]
     order = lax.broadcasted_iota(jnp.int32, (n_anchor, step_pix), 0)
     wanted = jnp.zeros((n_anchor, step_pix), jnp.int32)
@@ -299,7 +338,7 @@
     rows_half[...] = jnp.zeros_like(rows_half)
 
     def finish(j, carry):
-        value = gather(ITERS, j)
+        value = normal(gather(ITERS, j))
         slot = lo * chunks + j
         score[slot] = value
         send(score.at[slot], score.at[slot], sc_sem.at[j], (pix, mates[0])).start()
@@ -344,7 +383,7 @@
     n_hi = n_pix // GROUP
     vmem = pl.BlockSpec(memory_space=pltpu.VMEM)
     smem = pl.BlockSpec(memory_space=pltpu.SMEM)
-    hbm = pl.BlockSpec(memory_space=pl.ANY)
+    hbm = pl.BlockSpec(memory_space=pltpu.HBM)
     v = pltpu.VMEM
     sem = lambda *shape: pltpu.SemaphoreType.DMA(tuple(shape) + (2,))
     scratch = [
@@ -359,8 +398,9 @@
         v((ITERS, k // 2, 2 * k), F32), v((ITERS, 3, k // 2, 2 * k), F32),
         v((2 * chunks, k, step), F32), v((na, k), F32), v((na, k), F32), v((na, k), F32),
         v((n_pix, na, k), F32), v((192, 128), F32),
-        v((2 * k, 2 * ch), BF16), v((2 * k, pixels), BF16),
-        pltpu.SemaphoreType.DMA((2 * chunks,)), sem(), sem(), sem(n_pix), sem(3), sem(3), sem(ITERS + 1, chunks), sem(ITERS),
+        v((2 * k, 2 * ch), BF16), v((2 * k, step), BF16), v((k, 128), F32),
+        v((2 * k, pixels), BF16),
+        pltpu.SemaphoreType.DMA((2 * chunks,)), sem(chunks), sem(), sem(n_pix), sem(3), sem(3), sem(ITERS + 1, chunks), sem(ITERS),
         sem(ITERS, GROUP), sem(ITERS, n_hi), sem(ITERS, GROUP), sem(ITERS), sem(ITERS, 3),
         sem(chunks), sem(), sem(n_pix),
     ]
@@ -374,7 +414,7 @@
         out_specs=(vmem, vmem),
         scratch_shapes=scratch,
         compiler_params=pltpu.CompilerParams(
-            collective_id=0, has_side_effects=True, vmem_limit_bytes=60 * 1024 * 1024
+            collective_id=0, has_side_effects=True, vmem_limit_bytes=58 * 1024 * 1024
         ),
     )(spectra, start, anchors)
 

time: 163 us -> 149 us (0.914)
  Pallas kernels: 158 us -> 144 us
    pallas_call x1, Pallas kernels: 158 us -> 144 us  [local(): pl.pallas_call(functools.partial(kernel, n_pix), out_shape=(jax.ShapeDtyp...]
where the time goes in v5:
time: 149 us
  Pallas kernels  144 us (97%)
  local copies, waits for them, and re-layouts  3.94 us (3%)
    pallas_call x1, Pallas kernels, local(): pl.pallas_call(functools.partial(kernel, n_pix), out_shape=(jax.ShapeDtyp...  144 us
    unnamed x2, local copies, waits for them, and re-layouts  3.94 us

profile of v5, /device:TPU:0, one launch (start us, length us, event | category | flops | bytes accessed | tf_op | source)
XLA Modules:
  0.0 148.5 jit_solution(6308884890542981216)
XLA Ops:
  0.6 143.9 %shard_map.50 = (f32[64,4096]{1,0:T(8,128)}, f32[16,4096]{1,0:T(8,128)}) custom-call(bf16[4096,512]{1,0:T(8,128)(2,1)} %s_hbm.1, bf16[64,512]{1,0:T(8,128)(2,1)} %start_ref.1, s32[16]{0:T(128)} %anchors_ref.1), custom_call_target="tpu_custom_call" | custom-call | tf_op jit(solution)/shard_map/pallas_call | solution.py:407
  144.6 2.3 %copy.7 = f32[64,4096]{1,0:T(8,128)} copy(f32[64,4096]{1,0:T(8,128)} %get-tuple-element.4) | data formatting | bytes 2097152
  146.9 1.7 %copy.8 = f32[16,4096]{1,0:T(8,128)} copy(f32[16,4096]{1,0:T(8,128)} %get-tuple-element.5) | data formatting | bytes 524288

commit v6 on v5

--- a/solution.py
+++ b/solution.py
@@ -75,7 +75,8 @@
     s_ref, other_s, start_in, col_out, col_in, col_mine, col_chan, row_out, row_in, row_sum,
     w, wt, load, x_out, x_in, acc, half_in, keep, rs_in, hi_in, ag, back_in, padded,
     gram_out, gram_in, score, rows_half, rows_half_in, rows_out, rows_in, rows_pad,
-    halves, shares_split, factor_ref, pieces, in_sem, s_sem, st_sem, col_sem, cc_sem, row_sem, x_sem, half_sem, rs_sem, hi_sem, ag_sem,
+    halves, shares_split, factor_ref, pieces,
+    keep16, rs16, hi16, ag16, back16_in, pad16, in_sem, s_sem, st_sem, col_sem, cc_sem, row_sem, x_sem, half_sem, rs_sem, hi_sem, ag_sem,
     bk_sem, gram_sem, sc_sem, rh_sem, rows_sem,
 ):
     pix = lax.axis_index("pix")
@@ -179,6 +180,7 @@
     load[:, :ch] = start_ref[...]
     load[:, ch:] = start_in[...]
     padded[...] = jnp.zeros_like(padded)
+    pad16[...] = jnp.zeros_like(pad16)
     rows_pad[...] = jnp.zeros_like(rows_pad)
 
     def x_copy(t, j):
@@ -249,10 +251,99 @@
         copy = send(keep.at[t, 0], half_in.at[t], half_sem.at[t], (pix, mates[0]))
         copy.start()
         copy.wait()
+        if defer:
+            narrow(t)
+        else:
+            wide_sums(t)
+        return carry
+
+    def partner(d):
+        return lax.rem(low + d, GROUP)
+
+    def across_groups(t, slab, buffer):
+        if n_hi == 1:
+            return slab
+        buffer[t, 0] = slab
+        across = [
+            send(buffer.at[t, 0], buffer.at[t, e], hi_sem.at[t, e],
+                 (lax.rem(pix + e * GROUP, n_pix), chan))
+            for e in range(1, n_hi)
+        ]
+        for copy in across:
+            copy.start()
+        for copy in across:
+            copy.wait()
+        place = lax.div(pix, GROUP)
+        slab = buffer[t, lax.rem(n_hi + place, n_hi)]
+        for e in range(1, n_hi):
+            slab = slab + buffer[t, lax.rem(n_hi + place - e, n_hi)]
+        return slab
+
+    def gram_copies(t):
+        return [
+            send(gram_out.at[t], gram_in.at[t, m], gram_sem.at[t, m], (pix, mates[m]))
+            for m in range(3)
+        ]
+
+    def factor_of(t):
+        for copy in gram_copies(t):
+            copy.wait()
+        gram = (gram_out[t] + gram_in[t, 0]) + (gram_in[t, 1] + gram_in[t, 2])
+        return inverse_factor(
+            jnp.concatenate([pltpu.roll(gram, 64, 1), gram], axis=0))
+
+    slab_lanes = ch * k_rows // (16 * GROUP)
+    per_line = ch // slab_lanes
+
+    def slab_at(i):
+        return 16 * (i // per_line), (i % per_line) * slab_lanes
+
+    def narrow(t):
+        for i in range(GROUP):
+            r, c = slab_at(i)
+            part = acc[r : r + 16, c : c + slab_lanes]
+            part = part + half_in[t, r : r + 16, c : c + slab_lanes]
+            keep16[t, i] = part.astype(BF16)
+        spread = [
+            send(keep16.at[t, partner(d)], rs16.at[t, d], rs_sem.at[t, d],
+                 (base + partner(d), chan))
+            for d in range(1, GROUP)
+        ]
+        for copy in spread:
+            copy.start()
+        slab = keep16[t, low].astype(F32)
+        for d, copy in enumerate(spread, 1):
+            copy.wait()
+            slab = slab + rs16[t, d].astype(F32)
+        slab = across_groups(t, slab, hi16)
+        ag16[t, low] = slab.astype(BF16)
+        collect = [
+            send(ag16.at[t, low], ag16.at[t, low], ag_sem.at[t, d], (base + partner(d), chan))
+            for d in range(1, GROUP)
+        ]
+        for copy in collect:
+            copy.start()
+        for copy in collect:
+            copy.wait()
+        twin = send(ag16.at[t], back16_in.at[t], bk_sem.at[t], (pix, mates[0]))
+        twin.start()
+        for i in range(GROUP):
+            r, c = slab_at(i)
+            load[r : r + 16, c : c + slab_lanes] = ag16[t, i]
+            pad16[k_rows + r : k_rows + r + 16, c : c + slab_lanes] = ag16[t, i]
+        gram_out[t] = dot(load[: k_rows // 2, :ch], pad16[k_rows:, :], NT) + dot(
+            load[k_rows // 2 :, :ch], pad16[: 2 * k_rows, :], NT)
+        for copy in gram_copies(t):
+            copy.start()
+        twin.wait()
+        for i in range(GROUP):
+            r, c = slab_at(i)
+            load[r : r + 16, ch + c : ch + c + slab_lanes] = back16_in[t, i]
+        project(t + 1)
+        factor_ref[...] = factor_of(t)
+
+    def wide_sums(t):
         keep[t, 1] = acc[:, :ch] + half_in[t]
-
-        def partner(d):
-            return lax.rem(low + d, GROUP)
         spread = [
             send(
                 keep.at[t, 1, pl.ds(pl.multiple_of(partner(d) * per, per), per)],
@@ -265,20 +356,7 @@
         for d, copy in enumerate(spread, 1):
             copy.wait()
             slab = slab + rs_in[t, d]
-        if n_hi > 1:
-            hi_in[t, 0] = slab
-            across = [
-                send(hi_in.at[t, 0], hi_in.at[t, e], hi_sem.at[t, e],
-                     (lax.rem(pix + e * GROUP, n_pix), chan))
-                for e in range(1, n_hi)
-            ]
-            for copy in across:
-                copy.start()
-            for copy in across:
-                copy.wait()
-            slab = hi_in[t, lax.rem(n_hi + lax.div(pix, GROUP), n_hi)]
-            for e in range(1, n_hi):
-                slab = slab + hi_in[t, lax.rem(n_hi + lax.div(pix, GROUP) - e, n_hi)]
+        slab = across_groups(t, slab, hi_in)
         mine = pl.ds(pl.multiple_of(low * per, per), per)
         ag[t, mine] = slab
         collect = [
@@ -295,33 +373,15 @@
         padded[k_rows : 2 * k_rows, :] = back
         gram_out[t] = dot(back[: k_rows // 2], padded[k_rows:, :], NT, HIGH) + dot(
             back[k_rows // 2 :], padded[: 2 * k_rows, :], NT, HIGH)
-        grams = [
-            send(gram_out.at[t], gram_in.at[t, m], gram_sem.at[t, m], (pix, mates[m]))
-            for m in range(3)
-        ]
-        for copy in grams:
-            copy.start()
-        def factor_of():
-            for copy in grams:
-                copy.wait()
-            gram = (gram_out[t] + gram_in[t, 0]) + (gram_in[t, 1] + gram_in[t, 2])
-            return inverse_factor(
-                jnp.concatenate([pltpu.roll(gram, 64, 1), gram], axis=0))
-
-        if defer:
-            load[:, :ch] = back.astype(BF16)
-            twin.wait()
-            load[:, ch:] = back_in[t].astype(BF16)
-            project(t + 1)
-            factor_ref[...] = factor_of()
-        else:
-            split_rows(halves, back, slice(0, ch))
-            factor = factor_of()
-            twin.wait()
-            split_rows(halves, back_in[t], slice(ch, 2 * ch))
-            load[...] = split_dot(factor, halves[...]).astype(BF16)
-            project(t + 1)
-        return carry
+        for copy in gram_copies(t):
+            copy.start()
+        split_rows(halves, back, slice(0, ch))
+        factor = factor_of(t)
+        twin.wait()
+        split_rows(halves, back_in[t], slice(ch, 2 * ch))
+        load[...] = split_dot(factor, halves[...]).astype(BF16)
+        project(t + 1)
+
     plain = functools.partial(iteration, False, False)
     first = functools.partial(iteration, False, True)
     later = functools.partial(iteration, True, True)
@@ -386,6 +446,7 @@
     hbm = pl.BlockSpec(memory_space=pltpu.HBM)
     v = pltpu.VMEM
     sem = lambda *shape: pltpu.SemaphoreType.DMA(tuple(shape) + (2,))
+    slabs = lambda count, kind: v((ITERS, count, 16, ch * k // (16 * GROUP)), kind)
     scratch = [
         v((pixels, ch), BF16), v((half, ch), BF16), v((k, ch), BF16), v((1, ch), F32),
         v((n_pix, 1, ch), F32), v((1, ch), F32), v((3, 1, ch), F32), v((2 * chunks, step), F32),
@@ -400,6 +461,8 @@
         v((n_pix, na, k), F32), v((192, 128), F32),
         v((2 * k, 2 * ch), BF16), v((2 * k, step), BF16), v((k, 128), F32),
         v((2 * k, pixels), BF16),
+        slabs(GROUP, BF16), slabs(GROUP, BF16), slabs(n_hi, F32), slabs(GROUP, BF16),
+        slabs(GROUP, BF16), v((3 * k, ch), BF16),
         pltpu.SemaphoreType.DMA((2 * chunks,)), sem(chunks), sem(), sem(n_pix), sem(3), sem(3), sem(ITERS + 1, chunks), sem(ITERS),
         sem(ITERS, GROUP), sem(ITERS, n_hi), sem(ITERS, GROUP), sem(ITERS), sem(ITERS, 3),
         sem(chunks), sem(), sem(n_pix),
@@ -414,7 +477,7 @@
         out_specs=(vmem, vmem),
         scratch_shapes=scratch,
         compiler_params=pltpu.CompilerParams(
-            collective_id=0, has_side_effects=True, vmem_limit_bytes=58 * 1024 * 1024
+            collective_id=0, has_side_effects=True, vmem_limit_bytes=51 * 1024 * 1024
         ),
     )(spectra, start, anchors)
 

time: 149 us -> 142 us (0.953)
  Pallas kernels: 144 us -> 138 us
    pallas_call x1, Pallas kernels: 144 us -> 138 us  [local(): pl.pallas_call(functools.partial(kernel, n_pix), out_shape=(jax.ShapeDtyp...]
    unnamed x2 -> x6, local copies, waits for them, and re-layouts: 3.94 us -> 3.16 us
where the time goes in v6:
time: 142 us
  Pallas kernels  138 us (97%)
  local copies, waits for them, and re-layouts  3.16 us (2%)
    pallas_call x1, Pallas kernels, local(): pl.pallas_call(functools.partial(kernel, n_pix), out_shape=(jax.ShapeDtyp...  138 us
    unnamed x6, local copies, waits for them, and re-layouts  3.16 us

profile of v6, /device:TPU:0, one launch (start us, length us, event | category | flops | bytes accessed | tf_op | source)
XLA Modules:
  0.0 142.0 jit_solution(13594213514956551953)
XLA Ops:
  0.6 0.0 copy-start
  0.6 0.8 copy-done
  1.5 0.0 copy-start.1
  1.5 0.7 copy-done.1
  2.1 138.2 %shard_map.50 = (f32[64,4096]{1,0:T(8,128)S(1)}, f32[16,4096]{1,0:T(8,128)S(1)}) custom-call(bf16[4096,512]{1,0:T(8,128)(2,1)} %s_hbm.1, bf16[64,512]{1,0:T(8,128)(2,1)S(1)} %copy-done, s32[16]{0:T(128)S(1)} %copy-done.1), custom_call_target="tpu_custom_call" | custom-call | tf_op jit(solution)/shard_map/pallas_call | solution.py:470
  140.3 1.0 copy.7
  141.3 0.7 copy.8
Async XLA Ops:
  0.6 0.8 copy-start
  1.5 0.7 copy-start.1

commit v7 on v6

--- a/solution.py
+++ b/solution.py
@@ -403,8 +403,10 @@
         score[slot] = value
         send(score.at[slot], score.at[slot], sc_sem.at[j], (pix, mates[0])).start()
         positions = lax.broadcasted_iota(jnp.int32, (n_anchor, step_pix), 1)
-        picks = jnp.where(positions == wanted - j * step_pix, 1.0, 0.0)
-        rows_half[...] += dot(picks, value, NT, HIGH)
+        picks = jnp.where(positions == wanted - j * step_pix, 1.0, 0.0).astype(BF16)
+        top = value.astype(BF16)
+        rest = (value - top.astype(F32)).astype(BF16)
+        rows_half[...] += dot(picks, top, NT) + dot(picks, rest, NT)
         return carry
     lax.fori_loop(0, chunks, finish, 0)
     pair_rows = send(rows_half, rows_half_in, rh_sem, (pix, mates[0]))

time: 142 us -> 142 us (level)
  no operation moved by 1% of the time
where the time goes in v7:
time: 142 us
  Pallas kernels  138 us (97%)
  local copies, waits for them, and re-layouts  3.16 us (2%)
    pallas_call x1, Pallas kernels, local(): pl.pallas_call(functools.partial(kernel, n_pix), out_shape=(jax.ShapeDtyp...  138 us
    unnamed x6, local copies, waits for them, and re-layouts  3.16 us

profile of v7, /device:TPU:0, one launch (start us, length us, event | category | flops | bytes accessed | tf_op | source)
XLA Modules:
  0.0 141.9 jit_solution(7399334690319940746)
XLA Ops:
  0.6 0.0 copy-start
  0.6 0.8 copy-done
  1.5 0.0 copy-start.1
  1.5 0.7 copy-done.1
  2.1 138.1 %shard_map.50 = (f32[64,4096]{1,0:T(8,128)S(1)}, f32[16,4096]{1,0:T(8,128)S(1)}) custom-call(bf16[4096,512]{1,0:T(8,128)(2,1)} %s_hbm.1, bf16[64,512]{1,0:T(8,128)(2,1)S(1)} %copy-done, s32[16]{0:T(128)S(1)} %copy-done.1), custom_call_target="tpu_custom_call" | custom-call | tf_op jit(solution)/shard_map/pallas_call | solution.py:472
  140.2 1.0 copy.7
  141.2 0.7 copy.8
Async XLA Ops:
  0.6 0.8 copy-start
  1.5 0.7 copy-start.1
